TPU v7x, 128 devices: a whole 4x4x4 slice. The times are simulated.
128 devices in a mesh: gx: 8 (over x_hi, z), gy: 16 (over x_lo, y, core).
Axes of the slice: x: 4 (x_hi: 2, x_lo: 2; x = x_hi * 2 + x_lo), y: 4, z: 4, core: 2. Of those that a mesh axis runs over, the one named last changes fastest.
Arguments:
- object_field: float32 [2, 2, 1024, 2048], P(None, None, 'gx', 'gy'), may hold values from -1 to 1
- probe: float32 [2, 128, 128], replicated, may hold values from -0.5 to 0.5
- propagator: float32 [128, 128], replicated, may hold values from -3.140625 to 3.140625
- offsets: int32 [8, 16, 12, 2], P('gx', 'gy'), may hold values from 0 to 128
- counts: int32 [8, 16], P('gx', 'gy'), may hold values from 1 to 12, as said below
- intensity: float32 [8, 16, 12, 128, 128], P('gx', 'gy'), may hold values from 0.1 to 4
Outputs:
- updated_object: float32 [2, 2, 1024, 2048], P(None, None, 'gx', 'gy')
Inputs may be any that keep to these rules, and one draw needn't show every extreme that they name: `counts`: some tile has all 12 slots live in every draw; positions are live in slot order.
All inputs are finite; a program needn't handle non-finite values.
Results may differ from a plain program's by a relative error of at most 0.0003.
Values sent between devices are 32-bit elements; how exact they have to be, the bound alone decides.
A program may use at most 64 MiB of HBM per device.

v0:
```python
import math

import jax
import jax.numpy as jnp
from jax import lax
from jax.sharding import PartitionSpec as P

BATCH = 2
NB = 6


def shifted(block, axis, distance):
    devices = range(lax.axis_size(axis))
    route = [(i - distance, i) for i in devices if i - distance in devices]
    return lax.ppermute(block, axis, route)


def with_halo(value, sides, width):
    for axis, dim in sides:
        size, length = (lax.axis_size(axis), value.shape[dim])
        up = [(i, (i + 1) % size) for i in range(size - 1)]
        down = [(j, i) for i, j in up]
        last = lax.slice_in_dim(value, length - width, length, axis=dim)
        initial = lax.slice_in_dim(value, 0, width, axis=dim)
        before = lax.ppermute(last, axis, up)
        after = lax.ppermute(initial, axis, down)
        value = jnp.concatenate([before, value, after], axis=dim)
    return value


def product(first, second):
    return (
        first[0] * second[0] - first[1] * second[1],
        first[0] * second[1] + first[1] * second[0],
    )


def conjugate(field):
    return (field[0], -field[1])


def tables(width):
    index = jnp.arange(width, dtype=jnp.int32)
    phase = (index[:, None] * index[None, :] % width).astype(jnp.float32) * (2.0 * math.pi / width)
    return (jnp.cos(phase) / math.sqrt(width), jnp.sin(phase) / math.sqrt(width))


def left_mul(matrix, field):
    return jnp.einsum("ij,...jk->...ik", matrix, field, precision=lax.Precision.HIGHEST)


def right_mul(field, matrix):
    return jnp.einsum("...ij,jk->...ik", field, matrix, precision=lax.Precision.HIGHEST)


def transform(field, basis, direction):
    cosine = basis[0]
    signed = direction * basis[1]
    first_real = left_mul(cosine, field[0]) - left_mul(signed, field[1])
    first_imag = left_mul(cosine, field[1]) + left_mul(signed, field[0])
    return (
        right_mul(first_real, cosine) - right_mul(first_imag, signed),
        right_mul(first_imag, cosine) + right_mul(first_real, signed),
    )


def gradients(probe_pair, wave_pair, patches, measured, basis):
    slice_one = (patches[:, 0, 0], patches[:, 0, 1])
    slice_two = (patches[:, 1, 0], patches[:, 1, 1])
    entrance = product(probe_pair, slice_one)
    spectrum = product(transform(entrance, basis, -1.0), wave_pair)
    inner_wave = transform(spectrum, basis, 1.0)
    farfield = transform(product(inner_wave, slice_two), basis, -1.0)
    excess = farfield[0] * farfield[0] + farfield[1] * farfield[1] - measured
    back_exit = transform((excess * farfield[0], excess * farfield[1]), basis, 1.0)
    grad_two = product(conjugate(inner_wave), back_exit)
    back_inner = product(conjugate(slice_two), back_exit)
    back_spec = product(conjugate(wave_pair), transform(back_inner, basis, -1.0))
    grad_one = product(conjugate(probe_pair), transform(back_spec, basis, 1.0))
    return jnp.stack([jnp.stack(grad_one, 1), jnp.stack(grad_two, 1)], 1)


def settle(buffer, from_prior, from_next, margin, dim):
    length = buffer.shape[dim]
    inner = lax.slice_in_dim(buffer, margin, length - margin, axis=dim)
    middle = length - 2 * margin
    lower_part = lax.slice_in_dim(inner, 0, margin, axis=dim) + from_prior
    center = lax.slice_in_dim(inner, margin, middle - margin, axis=dim)
    upper_part = lax.slice_in_dim(inner, middle - margin, middle, axis=dim) + from_next
    return jnp.concatenate([lower_part, center, upper_part], axis=dim)


def fold_rows(buffer, margin):
    length = buffer.shape[2]
    upper_rim = lax.slice_in_dim(buffer, 0, margin, axis=2)
    lower_rim = lax.slice_in_dim(buffer, length - margin, length, axis=2)
    from_next = shifted(upper_rim, "gx", -1)
    from_prior = shifted(lower_rim, "gx", 1)
    return settle(buffer, from_prior, from_next, margin, 2)


def fold_cols(buffer, margin):
    length = buffer.shape[3]
    left_rim = lax.slice_in_dim(buffer, 0, margin, axis=3)
    right_rim = lax.slice_in_dim(buffer, length - margin, length, axis=3)
    from_next = shifted(left_rim, "gy", -1)
    from_prior = shifted(right_rim, "gy", 1)
    return settle(buffer, from_prior, from_next, margin, 3)


def local(object_field, probe, propagator, offsets, counts, intensity):
    width = probe.shape[1]
    margin = width // 2
    batch = BATCH
    basis = tables(width)
    probe_pair = (probe[0], probe[1])
    wave_pair = (jnp.cos(propagator), jnp.sin(propagator))
    zero = jnp.zeros((), jnp.int32)
    own_offsets = offsets[0, 0]
    own_intensity = intensity[0, 0]
    own_count = counts[0, 0]

    def period_step(period, field):
        padded = with_halo(field, (("gx", 2), ("gy", 3)), margin)
        first_slot = (period * batch).astype(jnp.int32)
        slot_offsets = lax.dynamic_slice_in_dim(own_offsets, first_slot, batch, 0)
        measured = lax.dynamic_slice_in_dim(own_intensity, first_slot, batch, 0)
        live = first_slot + jnp.arange(batch, dtype=jnp.int32) < own_count

        def take_patch(member):
            return lax.dynamic_slice(
                padded,
                (zero, zero, slot_offsets[member, 0], slot_offsets[member, 1]),
                (2, 2, width, width),
            )

        stacked = jnp.stack([take_patch(member) for member in range(batch)])
        grads = gradients(probe_pair, wave_pair, stacked, measured, basis)
        grads = grads * live.astype(jnp.float32)[:, None, None, None, None]

        def add_piece(member, total):
            place = (zero, zero, slot_offsets[member, 0], slot_offsets[member, 1])
            current = lax.dynamic_slice(total, place, (2, 2, width, width))
            return lax.dynamic_update_slice(total, current + grads[member], place)

        total = lax.fori_loop(0, batch, add_piece, jnp.zeros_like(padded))
        folded = fold_cols(fold_rows(total, margin), margin)
        return field - 0.08 * folded

    return lax.fori_loop(0, NB, period_step, object_field)


def solution(mesh):
    in_specs = (
        P(None, None, "gx", "gy"),
        P(),
        P(),
        P("gx", "gy", None, None),
        P("gx", "gy"),
        P("gx", "gy", None, None, None),
    )
    out_specs = P(None, None, "gx", "gy")
    return jax.shard_map(local, mesh=mesh, in_specs=in_specs, out_specs=out_specs, check_vma=False)
```

profile of v0, /device:TPU:6, one launch (start us, length us, event | category | flops | bytes accessed | tf_op | source)
XLA Modules:
  0.0 672.2 jit_solution(3348893015269683953)
XLA Ops:
  2.7 668.8 %while.51 = (s32[]{:T(128)}, f32[2,2,128,128]{3,2,1,0:T(8,128)S(1)}, s32[12,2]{0,1:T(2,128)S(1)}, f32[1,128,128]{2,1,0:T(8,128)S(1)}, f32[128,128]{1,0:T(8,128)S...) while((s32[]{:T(128)}, ...), condition=%wide.region_3.4_spmd.clone.clone, body=%wide.region_0.3_spmd.clone.clone.sunk | while | flops 2432237568 | bytes 44696700 | solution.py:150
  2.7 3.8 collective-permute-start
  6.5 5.6 collective-permute-start.1
  60.0 16.1 %while.52 = (s32[]{:T(128)}, f32[2,2,256,256]{3,2,1,0:T(8,128)S(1)}, s32[2,2]{1,0:T(2,128)S(1)}, f32[2,2,2,128,128]{4,3,0,2,1:T(8,128)S(1)}, s32[]{:T(128)}, /*index=5*/s32[]{:T(128)}, s32[]{:T(128)}) while((s32[]{:T(128)}, f32[2,2,256,256]{3,2,1,0:T(8,128)S(1)}, s32[2,2]{1,0:T(2,128)S(1)}, f32[2,2,2,128,128]{4,3,0,2,1:T(8,128)S(1)}, ...), condition=%wide.region_2.2_spmd, body=%wide.region_1.1_spmd.sunk | while | flops 65544 | bytes 1310901 | solution.py:146
  78.2 10.6 %collective-permute-done.4 = f32[2,2,64,256]{3,2,1,0:T(8,128)S(1)} collective-permute-done((f32[2,2,64,256]{3,2,1,0:T(8,128)S(1)}, f32[2,2,64,256]{3,2,1,0:T(8,128)S(1)}, u32[]{:S(2)}, u32[]{:S(2)}) %collective-permute-start.4) | collective-permute-done | bytes 262176 | tf_op jit(solution)/shard_map/while/body/eval_jaxpr/ppermute | solution.py:15
  92.7 4.5 collective-permute-done.5
  99.3 8.0 %collective-permute-done.6 = f32[2,2,128,64]{3,2,1,0:T(8,128)S(1)} collective-permute-done((f32[2,2,128,64]{3,2,1,0:T(8,128)S(1)}, f32[2,2,128,64]{3,2,1,0:T(8,128)S(1)}, u32[]{:S(2)}, u32[]{:S(2)}) %collective-permute-start.6) | collective-permute-done | bytes 131104 | tf_op jit(solution)/shard_map/while/body/eval_jaxpr/ppermute | solution.py:15
  109.4 3.9 collective-permute-done.7
  115.4 7.9 %collective-permute-start.1 = (f32[2,2,64,128]{3,2,1,0:T(8,128)S(1)}, f32[2,2,64,128]{3,2,1,0:T(8,128)S(1)}, u32[]{:S(2)}, u32[]{:S(2)}) collective-permute-start(f32[2,2,64,128]{3,2,1,0:T(8,128)S(1)} %get-tuple-element.832), channel_id=1, source_target_pairs={{16,0},{32,16},{48,32},{64,48},{80,64},{96,80},{112,96},{17,1},{33... | collective-permute-start | bytes 393224 | tf_op jit(solution)/shard_map/while/body/eval_jaxpr/ppermute | solution.py:26
  126.7 4.1 collective-permute-start.2
  172.4 16.1 %while.52 = (s32[]{:T(128)}, f32[2,2,256,256]{3,2,1,0:T(8,128)S(1)}, s32[2,2]{1,0:T(2,128)S(1)}, f32[2,2,2,128,128]{4,3,0,2,1:T(8,128)S(1)}, s32[]{:T(128)}, /*index=5*/s32[]{:T(128)}, s32[]{:T(128)}) while((s32[]{:T(128)}, f32[2,2,256,256]{3,2,1,0:T(8,128)S(1)}, s32[2,2]{1,0:T(2,128)S(1)}, f32[2,2,2,128,128]{4,3,0,2,1:T(8,128)S(1)}, ...), condition=%wide.region_2.2_spmd, body=%wide.region_1.1_spmd.sunk | while | flops 65544 | bytes 1310901 | solution.py:146
  190.5 10.4 %collective-permute-done.4 = f32[2,2,64,256]{3,2,1,0:T(8,128)S(1)} collective-permute-done((f32[2,2,64,256]{3,2,1,0:T(8,128)S(1)}, f32[2,2,64,256]{3,2,1,0:T(8,128)S(1)}, u32[]{:S(2)}, u32[]{:S(2)}) %collective-permute-start.4) | collective-permute-done | bytes 262176 | tf_op jit(solution)/shard_map/while/body/eval_jaxpr/ppermute | solution.py:15
  201.0 3.9 collective-permute-start.5
  204.9 4.3 collective-permute-done.5
  211.4 7.9 %collective-permute-done.6 = f32[2,2,128,64]{3,2,1,0:T(8,128)S(1)} collective-permute-done((f32[2,2,128,64]{3,2,1,0:T(8,128)S(1)}, f32[2,2,128,64]{3,2,1,0:T(8,128)S(1)}, u32[]{:S(2)}, u32[]{:S(2)}) %collective-permute-start.6) | collective-permute-done | bytes 131104 | tf_op jit(solution)/shard_map/while/body/eval_jaxpr/ppermute | solution.py:15
  221.3 3.9 collective-permute-done.7
  227.4 7.5 %collective-permute-start.1 = (f32[2,2,64,128]{3,2,1,0:T(8,128)S(1)}, f32[2,2,64,128]{3,2,1,0:T(8,128)S(1)}, u32[]{:S(2)}, u32[]{:S(2)}) collective-permute-start(f32[2,2,64,128]{3,2,1,0:T(8,128)S(1)} %get-tuple-element.832), channel_id=1, source_target_pairs={{16,0},{32,16},{48,32},{64,48},{80,64},{96,80},{112,96},{17,1},{33... | collective-permute-start | bytes 393224 | tf_op jit(solution)/shard_map/while/body/eval_jaxpr/ppermute | solution.py:26
  237.7 4.7 collective-permute-start.2
  284.0 15.9 %while.52 = (s32[]{:T(128)}, f32[2,2,256,256]{3,2,1,0:T(8,128)S(1)}, s32[2,2]{1,0:T(2,128)S(1)}, f32[2,2,2,128,128]{4,3,0,2,1:T(8,128)S(1)}, s32[]{:T(128)}, /*index=5*/s32[]{:T(128)}, s32[]{:T(128)}) while((s32[]{:T(128)}, f32[2,2,256,256]{3,2,1,0:T(8,128)S(1)}, s32[2,2]{1,0:T(2,128)S(1)}, f32[2,2,2,128,128]{4,3,0,2,1:T(8,128)S(1)}, ...), condition=%wide.region_2.2_spmd, body=%wide.region_1.1_spmd.sunk | while | flops 65544 | bytes 1310901 | solution.py:146
  301.8 10.5 %collective-permute-done.4 = f32[2,2,64,256]{3,2,1,0:T(8,128)S(1)} collective-permute-done((f32[2,2,64,256]{3,2,1,0:T(8,128)S(1)}, f32[2,2,64,256]{3,2,1,0:T(8,128)S(1)}, u32[]{:S(2)}, u32[]{:S(2)}) %collective-permute-start.4) | collective-permute-done | bytes 262176 | tf_op jit(solution)/shard_map/while/body/eval_jaxpr/ppermute | solution.py:15
  312.4 3.9 collective-permute-start.5
  316.3 4.3 collective-permute-done.5
  322.8 7.9 %collective-permute-done.6 = f32[2,2,128,64]{3,2,1,0:T(8,128)S(1)} collective-permute-done((f32[2,2,128,64]{3,2,1,0:T(8,128)S(1)}, f32[2,2,128,64]{3,2,1,0:T(8,128)S(1)}, u32[]{:S(2)}, u32[]{:S(2)}) %collective-permute-start.6) | collective-permute-done | bytes 131104 | tf_op jit(solution)/shard_map/while/body/eval_jaxpr/ppermute | solution.py:15
  332.7 3.9 collective-permute-done.7
  338.7 7.5 %collective-permute-start.1 = (f32[2,2,64,128]{3,2,1,0:T(8,128)S(1)}, f32[2,2,64,128]{3,2,1,0:T(8,128)S(1)}, u32[]{:S(2)}, u32[]{:S(2)}) collective-permute-start(f32[2,2,64,128]{3,2,1,0:T(8,128)S(1)} %get-tuple-element.832), channel_id=1, source_target_pairs={{16,0},{32,16},{48,32},{64,48},{80,64},{96,80},{112,96},{17,1},{33... | collective-permute-start | bytes 393224 | tf_op jit(solution)/shard_map/while/body/eval_jaxpr/ppermute | solution.py:26
  349.0 4.8 collective-permute-start.2
  395.4 16.1 %while.52 = (s32[]{:T(128)}, f32[2,2,256,256]{3,2,1,0:T(8,128)S(1)}, s32[2,2]{1,0:T(2,128)S(1)}, f32[2,2,2,128,128]{4,3,0,2,1:T(8,128)S(1)}, s32[]{:T(128)}, /*index=5*/s32[]{:T(128)}, s32[]{:T(128)}) while((s32[]{:T(128)}, f32[2,2,256,256]{3,2,1,0:T(8,128)S(1)}, s32[2,2]{1,0:T(2,128)S(1)}, f32[2,2,2,128,128]{4,3,0,2,1:T(8,128)S(1)}, ...), condition=%wide.region_2.2_spmd, body=%wide.region_1.1_spmd.sunk | while | flops 65544 | bytes 1310901 | solution.py:146
  413.4 10.5 %collective-permute-done.4 = f32[2,2,64,256]{3,2,1,0:T(8,128)S(1)} collective-permute-done((f32[2,2,64,256]{3,2,1,0:T(8,128)S(1)}, f32[2,2,64,256]{3,2,1,0:T(8,128)S(1)}, u32[]{:S(2)}, u32[]{:S(2)}) %collective-permute-start.4) | collective-permute-done | bytes 262176 | tf_op jit(solution)/shard_map/while/body/eval_jaxpr/ppermute | solution.py:15
  424.0 3.9 collective-permute-start.5
  428.0 4.3 collective-permute-done.5
  434.4 7.9 %collective-permute-done.6 = f32[2,2,128,64]{3,2,1,0:T(8,128)S(1)} collective-permute-done((f32[2,2,128,64]{3,2,1,0:T(8,128)S(1)}, f32[2,2,128,64]{3,2,1,0:T(8,128)S(1)}, u32[]{:S(2)}, u32[]{:S(2)}) %collective-permute-start.6) | collective-permute-done | bytes 131104 | tf_op jit(solution)/shard_map/while/body/eval_jaxpr/ppermute | solution.py:15
  444.3 3.9 collective-permute-done.7
  450.4 7.5 %collective-permute-start.1 = (f32[2,2,64,128]{3,2,1,0:T(8,128)S(1)}, f32[2,2,64,128]{3,2,1,0:T(8,128)S(1)}, u32[]{:S(2)}, u32[]{:S(2)}) collective-permute-start(f32[2,2,64,128]{3,2,1,0:T(8,128)S(1)} %get-tuple-element.832), channel_id=1, source_target_pairs={{16,0},{32,16},{48,32},{64,48},{80,64},{96,80},{112,96},{17,1},{33... | collective-permute-start | bytes 393224 | tf_op jit(solution)/shard_map/while/body/eval_jaxpr/ppermute | solution.py:26
  460.7 4.8 collective-permute-start.2
  507.0 16.0 %while.52 = (s32[]{:T(128)}, f32[2,2,256,256]{3,2,1,0:T(8,128)S(1)}, s32[2,2]{1,0:T(2,128)S(1)}, f32[2,2,2,128,128]{4,3,0,2,1:T(8,128)S(1)}, s32[]{:T(128)}, /*index=5*/s32[]{:T(128)}, s32[]{:T(128)}) while((s32[]{:T(128)}, f32[2,2,256,256]{3,2,1,0:T(8,128)S(1)}, s32[2,2]{1,0:T(2,128)S(1)}, f32[2,2,2,128,128]{4,3,0,2,1:T(8,128)S(1)}, ...), condition=%wide.region_2.2_spmd, body=%wide.region_1.1_spmd.sunk | while | flops 65544 | bytes 1310901 | solution.py:146
  525.0 10.5 %collective-permute-done.4 = f32[2,2,64,256]{3,2,1,0:T(8,128)S(1)} collective-permute-done((f32[2,2,64,256]{3,2,1,0:T(8,128)S(1)}, f32[2,2,64,256]{3,2,1,0:T(8,128)S(1)}, u32[]{:S(2)}, u32[]{:S(2)}) %collective-permute-start.4) | collective-permute-done | bytes 262176 | tf_op jit(solution)/shard_map/while/body/eval_jaxpr/ppermute | solution.py:15
  535.6 3.9 collective-permute-start.5
  539.5 4.3 collective-permute-done.5
  546.0 7.9 %collective-permute-done.6 = f32[2,2,128,64]{3,2,1,0:T(8,128)S(1)} collective-permute-done((f32[2,2,128,64]{3,2,1,0:T(8,128)S(1)}, f32[2,2,128,64]{3,2,1,0:T(8,128)S(1)}, u32[]{:S(2)}, u32[]{:S(2)}) %collective-permute-start.6) | collective-permute-done | bytes 131104 | tf_op jit(solution)/shard_map/while/body/eval_jaxpr/ppermute | solution.py:15
  555.9 3.9 collective-permute-done.7
  562.0 7.5 %collective-permute-start.1 = (f32[2,2,64,128]{3,2,1,0:T(8,128)S(1)}, f32[2,2,64,128]{3,2,1,0:T(8,128)S(1)}, u32[]{:S(2)}, u32[]{:S(2)}) collective-permute-start(f32[2,2,64,128]{3,2,1,0:T(8,128)S(1)} %get-tuple-element.832), channel_id=1, source_target_pairs={{16,0},{32,16},{48,32},{64,48},{80,64},{96,80},{112,96},{17,1},{33... | collective-permute-start | bytes 393224 | tf_op jit(solution)/shard_map/while/body/eval_jaxpr/ppermute | solution.py:26
  572.2 4.8 collective-permute-start.2
  618.6 16.0 %while.52 = (s32[]{:T(128)}, f32[2,2,256,256]{3,2,1,0:T(8,128)S(1)}, s32[2,2]{1,0:T(2,128)S(1)}, f32[2,2,2,128,128]{4,3,0,2,1:T(8,128)S(1)}, s32[]{:T(128)}, /*index=5*/s32[]{:T(128)}, s32[]{:T(128)}) while((s32[]{:T(128)}, f32[2,2,256,256]{3,2,1,0:T(8,128)S(1)}, s32[2,2]{1,0:T(2,128)S(1)}, f32[2,2,2,128,128]{4,3,0,2,1:T(8,128)S(1)}, ...), condition=%wide.region_2.2_spmd, body=%wide.region_1.1_spmd.sunk | while | flops 65544 | bytes 1310901 | solution.py:146
  636.6 10.5 %collective-permute-done.4 = f32[2,2,64,256]{3,2,1,0:T(8,128)S(1)} collective-permute-done((f32[2,2,64,256]{3,2,1,0:T(8,128)S(1)}, f32[2,2,64,256]{3,2,1,0:T(8,128)S(1)}, u32[]{:S(2)}, u32[]{:S(2)}) %collective-permute-start.4) | collective-permute-done | bytes 262176 | tf_op jit(solution)/shard_map/while/body/eval_jaxpr/ppermute | solution.py:15
  647.1 3.9 collective-permute-start.5
  651.0 4.3 collective-permute-done.5
  657.5 7.9 %collective-permute-done.6 = f32[2,2,128,64]{3,2,1,0:T(8,128)S(1)} collective-permute-done((f32[2,2,128,64]{3,2,1,0:T(8,128)S(1)}, f32[2,2,128,64]{3,2,1,0:T(8,128)S(1)}, u32[]{:S(2)}, u32[]{:S(2)}) %collective-permute-start.6) | collective-permute-done | bytes 131104 | tf_op jit(solution)/shard_map/while/body/eval_jaxpr/ppermute | solution.py:15
  667.4 3.9 collective-permute-done.7
  (536 shorter events, 326.4 us)
Async XLA Ops:
  2.7 10.7 %collective-permute-start = (f32[2,2,64,128]{3,2,1,0:T(8,128)S(1)}, f32[2,2,64,128]{3,2,1,0:T(8,128)S(1)}, u32[]{:S(2)}, u32[]{:S(2)}) collective-permute-start(f32[2,2,64,128]{3,2,1,0:T(8,128)S(1)} %get-tuple-element.831), channel_id=1, source_target_pairs={{0,16},{16,32},{32,48},{48,64},{64,80},{80,96},{96,112},{1,17},{17... | collective-permute-start | bytes 393224 | tf_op jit(solution)/shard_map/while/body/eval_jaxpr/ppermute | solution.py:25
  6.5 8.1 %collective-permute-start.1 = (f32[2,2,64,128]{3,2,1,0:T(8,128)S(1)}, f32[2,2,64,128]{3,2,1,0:T(8,128)S(1)}, u32[]{:S(2)}, u32[]{:S(2)}) collective-permute-start(f32[2,2,64,128]{3,2,1,0:T(8,128)S(1)} %get-tuple-element.832), channel_id=1, source_target_pairs={{16,0},{32,16},{48,32},{64,48},{80,64},{96,80},{112,96},{17,1},{33... | collective-permute-start | bytes 393224 | tf_op jit(solution)/shard_map/while/body/eval_jaxpr/ppermute | solution.py:26
  14.9 14.4 %collective-permute-start.2 = (f32[2,2,256,64]{3,2,1,0:T(8,128)S(1)}, f32[2,2,256,64]{3,2,1,0:T(8,128)S(1)}, u32[]{:S(2)}, u32[]{:S(2)}) collective-permute-start(f32[2,2,256,64]{3,2,1,0:T(8,128)S(1)} %get-tuple-element.833), channel_id=1, source_target_pairs={{1,0},{2,1},{3,2},{4,3},{5,4},{6,5},{7,6},{8,7},{9,8},{10,9},{11,1... | collective-permute-start | bytes 786440 | tf_op jit(solution)/shard_map/while/body/eval_jaxpr/ppermute | solution.py:26
  18.4 12.6 %collective-permute-start.3 = (f32[2,2,256,64]{3,2,1,0:T(8,128)S(1)}, f32[2,2,256,64]{3,2,1,0:T(8,128)S(1)}, u32[]{:S(2)}, u32[]{:S(2)}) collective-permute-start(f32[2,2,256,64]{3,2,1,0:T(8,128)S(1)} %get-tuple-element.834), channel_id=1, source_target_pairs={{0,1},{1,2},{2,3},{3,4},{4,5},{5,6},{6,7},{7,8},{8,9},{9,10},{10,1... | collective-permute-start | bytes 786440 | tf_op jit(solution)/shard_map/while/body/eval_jaxpr/ppermute | solution.py:25
  76.1 12.7 %collective-permute-start.4 = (f32[2,2,64,256]{3,2,1,0:T(8,128)S(1)}, f32[2,2,64,256]{3,2,1,0:T(8,128)S(1)}, u32[]{:S(2)}, u32[]{:S(2)}) collective-permute-start(f32[2,2,64,256]{3,2,1,0:T(8,128)S(1)} %slice.373), channel_id=1, source_target_pairs={{0,16},{16,32},{32,48},{48,64},{64,80},{80,96},{96,112},{1,17},{17... | collective-permute-start | bytes 786440 | tf_op jit(solution)/shard_map/while/body/eval_jaxpr/ppermute | solution.py:15
  88.9 8.3 %collective-permute-start.5 = (f32[2,2,64,256]{3,2,1,0:T(8,128)S(1)}, f32[2,2,64,256]{3,2,1,0:T(8,128)S(1)}, u32[]{:S(2)}, u32[]{:S(2)}) collective-permute-start(f32[2,2,64,256]{3,2,1,0:T(8,128)S(1)} %get-tuple-element.858), channel_id=1, source_target_pairs={{16,0},{32,16},{48,32},{64,48},{80,64},{96,80},{112,96},{17,1},{33... | collective-permute-start | bytes 786440 | tf_op jit(solution)/shard_map/while/body/eval_jaxpr/ppermute | solution.py:15
  97.4 9.9 %collective-permute-start.6 = (f32[2,2,128,64]{3,2,1,0:T(8,128)S(1)}, f32[2,2,128,64]{3,2,1,0:T(8,128)S(1)}, u32[]{:S(2)}, u32[]{:S(2)}) collective-permute-start(f32[2,2,128,64]{3,2,1,0:T(8,128)S(1)} %fusion.646), channel_id=1, source_target_pairs={{0,1},{1,2},{2,3},{3,4},{4,5},{5,6},{6,7},{7,8},{8,9},{9,10},{10,1... | collective-permute-start | bytes 393224 | tf_op jit(solution)/shard_map/while/body/eval_jaxpr/ppermute | solution.py:15
  107.4 5.8 collective-permute-start.7
  113.5 11.8 %collective-permute-start = (f32[2,2,64,128]{3,2,1,0:T(8,128)S(1)}, f32[2,2,64,128]{3,2,1,0:T(8,128)S(1)}, u32[]{:S(2)}, u32[]{:S(2)}) collective-permute-start(f32[2,2,64,128]{3,2,1,0:T(8,128)S(1)} %get-tuple-element.831), channel_id=1, source_target_pairs={{0,16},{16,32},{32,48},{48,64},{64,80},{80,96},{96,112},{1,17},{17... | collective-permute-start | bytes 393224 | tf_op jit(solution)/shard_map/while/body/eval_jaxpr/ppermute | solution.py:25
  115.4 11.1 %collective-permute-start.1 = (f32[2,2,64,128]{3,2,1,0:T(8,128)S(1)}, f32[2,2,64,128]{3,2,1,0:T(8,128)S(1)}, u32[]{:S(2)}, u32[]{:S(2)}) collective-permute-start(f32[2,2,64,128]{3,2,1,0:T(8,128)S(1)} %get-tuple-element.832), channel_id=1, source_target_pairs={{16,0},{32,16},{48,32},{64,48},{80,64},{96,80},{112,96},{17,1},{33... | collective-permute-start | bytes 393224 | tf_op jit(solution)/shard_map/while/body/eval_jaxpr/ppermute | solution.py:26
  126.7 15.1 %collective-permute-start.2 = (f32[2,2,256,64]{3,2,1,0:T(8,128)S(1)}, f32[2,2,256,64]{3,2,1,0:T(8,128)S(1)}, u32[]{:S(2)}, u32[]{:S(2)}) collective-permute-start(f32[2,2,256,64]{3,2,1,0:T(8,128)S(1)} %get-tuple-element.833), channel_id=1, source_target_pairs={{1,0},{2,1},{3,2},{4,3},{5,4},{6,5},{7,6},{8,7},{9,8},{10,9},{11,1... | collective-permute-start | bytes 786440 | tf_op jit(solution)/shard_map/while/body/eval_jaxpr/ppermute | solution.py:26
  130.8 12.6 %collective-permute-start.3 = (f32[2,2,256,64]{3,2,1,0:T(8,128)S(1)}, f32[2,2,256,64]{3,2,1,0:T(8,128)S(1)}, u32[]{:S(2)}, u32[]{:S(2)}) collective-permute-start(f32[2,2,256,64]{3,2,1,0:T(8,128)S(1)} %get-tuple-element.834), channel_id=1, source_target_pairs={{0,1},{1,2},{2,3},{3,4},{4,5},{5,6},{6,7},{7,8},{8,9},{9,10},{10,1... | collective-permute-start | bytes 786440 | tf_op jit(solution)/shard_map/while/body/eval_jaxpr/ppermute | solution.py:25
  188.6 12.3 %collective-permute-start.4 = (f32[2,2,64,256]{3,2,1,0:T(8,128)S(1)}, f32[2,2,64,256]{3,2,1,0:T(8,128)S(1)}, u32[]{:S(2)}, u32[]{:S(2)}) collective-permute-start(f32[2,2,64,256]{3,2,1,0:T(8,128)S(1)} %slice.373), channel_id=1, source_target_pairs={{0,16},{16,32},{32,48},{48,64},{64,80},{80,96},{96,112},{1,17},{17... | collective-permute-start | bytes 786440 | tf_op jit(solution)/shard_map/while/body/eval_jaxpr/ppermute | solution.py:15
  201.0 8.3 %collective-permute-start.5 = (f32[2,2,64,256]{3,2,1,0:T(8,128)S(1)}, f32[2,2,64,256]{3,2,1,0:T(8,128)S(1)}, u32[]{:S(2)}, u32[]{:S(2)}) collective-permute-start(f32[2,2,64,256]{3,2,1,0:T(8,128)S(1)} %get-tuple-element.858), channel_id=1, source_target_pairs={{16,0},{32,16},{48,32},{64,48},{80,64},{96,80},{112,96},{17,1},{33... | collective-permute-start | bytes 786440 | tf_op jit(solution)/shard_map/while/body/eval_jaxpr/ppermute | solution.py:15
  209.4 9.8 %collective-permute-start.6 = (f32[2,2,128,64]{3,2,1,0:T(8,128)S(1)}, f32[2,2,128,64]{3,2,1,0:T(8,128)S(1)}, u32[]{:S(2)}, u32[]{:S(2)}) collective-permute-start(f32[2,2,128,64]{3,2,1,0:T(8,128)S(1)} %fusion.646), channel_id=1, source_target_pairs={{0,1},{1,2},{2,3},{3,4},{4,5},{5,6},{6,7},{7,8},{8,9},{9,10},{10,1... | collective-permute-start | bytes 393224 | tf_op jit(solution)/shard_map/while/body/eval_jaxpr/ppermute | solution.py:15
  219.4 5.8 collective-permute-start.7
  225.4 10.9 %collective-permute-start = (f32[2,2,64,128]{3,2,1,0:T(8,128)S(1)}, f32[2,2,64,128]{3,2,1,0:T(8,128)S(1)}, u32[]{:S(2)}, u32[]{:S(2)}) collective-permute-start(f32[2,2,64,128]{3,2,1,0:T(8,128)S(1)} %get-tuple-element.831), channel_id=1, source_target_pairs={{0,16},{16,32},{32,48},{48,64},{64,80},{80,96},{96,112},{1,17},{17... | collective-permute-start | bytes 393224 | tf_op jit(solution)/shard_map/while/body/eval_jaxpr/ppermute | solution.py:25
  227.4 10.1 %collective-permute-start.1 = (f32[2,2,64,128]{3,2,1,0:T(8,128)S(1)}, f32[2,2,64,128]{3,2,1,0:T(8,128)S(1)}, u32[]{:S(2)}, u32[]{:S(2)}) collective-permute-start(f32[2,2,64,128]{3,2,1,0:T(8,128)S(1)} %get-tuple-element.832), channel_id=1, source_target_pairs={{16,0},{32,16},{48,32},{64,48},{80,64},{96,80},{112,96},{17,1},{33... | collective-permute-start | bytes 393224 | tf_op jit(solution)/shard_map/while/body/eval_jaxpr/ppermute | solution.py:26
  237.7 15.7 %collective-permute-start.2 = (f32[2,2,256,64]{3,2,1,0:T(8,128)S(1)}, f32[2,2,256,64]{3,2,1,0:T(8,128)S(1)}, u32[]{:S(2)}, u32[]{:S(2)}) collective-permute-start(f32[2,2,256,64]{3,2,1,0:T(8,128)S(1)} %get-tuple-element.833), channel_id=1, source_target_pairs={{1,0},{2,1},{3,2},{4,3},{5,4},{6,5},{7,6},{8,7},{9,8},{10,9},{11,1... | collective-permute-start | bytes 786440 | tf_op jit(solution)/shard_map/while/body/eval_jaxpr/ppermute | solution.py:26
  242.4 12.6 %collective-permute-start.3 = (f32[2,2,256,64]{3,2,1,0:T(8,128)S(1)}, f32[2,2,256,64]{3,2,1,0:T(8,128)S(1)}, u32[]{:S(2)}, u32[]{:S(2)}) collective-permute-start(f32[2,2,256,64]{3,2,1,0:T(8,128)S(1)} %get-tuple-element.834), channel_id=1, source_target_pairs={{0,1},{1,2},{2,3},{3,4},{4,5},{5,6},{6,7},{7,8},{8,9},{9,10},{10,1... | collective-permute-start | bytes 786440 | tf_op jit(solution)/shard_map/while/body/eval_jaxpr/ppermute | solution.py:25
  299.9 12.4 %collective-permute-start.4 = (f32[2,2,64,256]{3,2,1,0:T(8,128)S(1)}, f32[2,2,64,256]{3,2,1,0:T(8,128)S(1)}, u32[]{:S(2)}, u32[]{:S(2)}) collective-permute-start(f32[2,2,64,256]{3,2,1,0:T(8,128)S(1)} %slice.373), channel_id=1, source_target_pairs={{0,16},{16,32},{32,48},{48,64},{64,80},{80,96},{96,112},{1,17},{17... | collective-permute-start | bytes 786440 | tf_op jit(solution)/shard_map/while/body/eval_jaxpr/ppermute | solution.py:15
  312.4 8.3 %collective-permute-start.5 = (f32[2,2,64,256]{3,2,1,0:T(8,128)S(1)}, f32[2,2,64,256]{3,2,1,0:T(8,128)S(1)}, u32[]{:S(2)}, u32[]{:S(2)}) collective-permute-start(f32[2,2,64,256]{3,2,1,0:T(8,128)S(1)} %get-tuple-element.858), channel_id=1, source_target_pairs={{16,0},{32,16},{48,32},{64,48},{80,64},{96,80},{112,96},{17,1},{33... | collective-permute-start | bytes 786440 | tf_op jit(solution)/shard_map/while/body/eval_jaxpr/ppermute | solution.py:15
  320.8 9.8 %collective-permute-start.6 = (f32[2,2,128,64]{3,2,1,0:T(8,128)S(1)}, f32[2,2,128,64]{3,2,1,0:T(8,128)S(1)}, u32[]{:S(2)}, u32[]{:S(2)}) collective-permute-start(f32[2,2,128,64]{3,2,1,0:T(8,128)S(1)} %fusion.646), channel_id=1, source_target_pairs={{0,1},{1,2},{2,3},{3,4},{4,5},{5,6},{6,7},{7,8},{8,9},{9,10},{10,1... | collective-permute-start | bytes 393224 | tf_op jit(solution)/shard_map/while/body/eval_jaxpr/ppermute | solution.py:15
  330.8 5.8 collective-permute-start.7
  336.8 10.5 %collective-permute-start = (f32[2,2,64,128]{3,2,1,0:T(8,128)S(1)}, f32[2,2,64,128]{3,2,1,0:T(8,128)S(1)}, u32[]{:S(2)}, u32[]{:S(2)}) collective-permute-start(f32[2,2,64,128]{3,2,1,0:T(8,128)S(1)} %get-tuple-element.831), channel_id=1, source_target_pairs={{0,16},{16,32},{32,48},{48,64},{64,80},{80,96},{96,112},{1,17},{17... | collective-permute-start | bytes 393224 | tf_op jit(solution)/shard_map/while/body/eval_jaxpr/ppermute | solution.py:25
  338.7 10.0 %collective-permute-start.1 = (f32[2,2,64,128]{3,2,1,0:T(8,128)S(1)}, f32[2,2,64,128]{3,2,1,0:T(8,128)S(1)}, u32[]{:S(2)}, u32[]{:S(2)}) collective-permute-start(f32[2,2,64,128]{3,2,1,0:T(8,128)S(1)} %get-tuple-element.832), channel_id=1, source_target_pairs={{16,0},{32,16},{48,32},{64,48},{80,64},{96,80},{112,96},{17,1},{33... | collective-permute-start | bytes 393224 | tf_op jit(solution)/shard_map/while/body/eval_jaxpr/ppermute | solution.py:26
  349.0 15.7 %collective-permute-start.2 = (f32[2,2,256,64]{3,2,1,0:T(8,128)S(1)}, f32[2,2,256,64]{3,2,1,0:T(8,128)S(1)}, u32[]{:S(2)}, u32[]{:S(2)}) collective-permute-start(f32[2,2,256,64]{3,2,1,0:T(8,128)S(1)} %get-tuple-element.833), channel_id=1, source_target_pairs={{1,0},{2,1},{3,2},{4,3},{5,4},{6,5},{7,6},{8,7},{9,8},{10,9},{11,1... | collective-permute-start | bytes 786440 | tf_op jit(solution)/shard_map/while/body/eval_jaxpr/ppermute | solution.py:26
  353.8 12.6 %collective-permute-start.3 = (f32[2,2,256,64]{3,2,1,0:T(8,128)S(1)}, f32[2,2,256,64]{3,2,1,0:T(8,128)S(1)}, u32[]{:S(2)}, u32[]{:S(2)}) collective-permute-start(f32[2,2,256,64]{3,2,1,0:T(8,128)S(1)} %get-tuple-element.834), channel_id=1, source_target_pairs={{0,1},{1,2},{2,3},{3,4},{4,5},{5,6},{6,7},{7,8},{8,9},{9,10},{10,1... | collective-permute-start | bytes 786440 | tf_op jit(solution)/shard_map/while/body/eval_jaxpr/ppermute | solution.py:25
  411.5 12.5 %collective-permute-start.4 = (f32[2,2,64,256]{3,2,1,0:T(8,128)S(1)}, f32[2,2,64,256]{3,2,1,0:T(8,128)S(1)}, u32[]{:S(2)}, u32[]{:S(2)}) collective-permute-start(f32[2,2,64,256]{3,2,1,0:T(8,128)S(1)} %slice.373), channel_id=1, source_target_pairs={{0,16},{16,32},{32,48},{48,64},{64,80},{80,96},{96,112},{1,17},{17... | collective-permute-start | bytes 786440 | tf_op jit(solution)/shard_map/while/body/eval_jaxpr/ppermute | solution.py:15
  424.0 8.3 %collective-permute-start.5 = (f32[2,2,64,256]{3,2,1,0:T(8,128)S(1)}, f32[2,2,64,256]{3,2,1,0:T(8,128)S(1)}, u32[]{:S(2)}, u32[]{:S(2)}) collective-permute-start(f32[2,2,64,256]{3,2,1,0:T(8,128)S(1)} %get-tuple-element.858), channel_id=1, source_target_pairs={{16,0},{32,16},{48,32},{64,48},{80,64},{96,80},{112,96},{17,1},{33... | collective-permute-start | bytes 786440 | tf_op jit(solution)/shard_map/while/body/eval_jaxpr/ppermute | solution.py:15
  432.5 9.8 %collective-permute-start.6 = (f32[2,2,128,64]{3,2,1,0:T(8,128)S(1)}, f32[2,2,128,64]{3,2,1,0:T(8,128)S(1)}, u32[]{:S(2)}, u32[]{:S(2)}) collective-permute-start(f32[2,2,128,64]{3,2,1,0:T(8,128)S(1)} %fusion.646), channel_id=1, source_target_pairs={{0,1},{1,2},{2,3},{3,4},{4,5},{5,6},{6,7},{7,8},{8,9},{9,10},{10,1... | collective-permute-start | bytes 393224 | tf_op jit(solution)/shard_map/while/body/eval_jaxpr/ppermute | solution.py:15
  442.4 5.8 collective-permute-start.7
  448.5 10.5 %collective-permute-start = (f32[2,2,64,128]{3,2,1,0:T(8,128)S(1)}, f32[2,2,64,128]{3,2,1,0:T(8,128)S(1)}, u32[]{:S(2)}, u32[]{:S(2)}) collective-permute-start(f32[2,2,64,128]{3,2,1,0:T(8,128)S(1)} %get-tuple-element.831), channel_id=1, source_target_pairs={{0,16},{16,32},{32,48},{48,64},{64,80},{80,96},{96,112},{1,17},{17... | collective-permute-start | bytes 393224 | tf_op jit(solution)/shard_map/while/body/eval_jaxpr/ppermute | solution.py:25
  450.4 10.0 %collective-permute-start.1 = (f32[2,2,64,128]{3,2,1,0:T(8,128)S(1)}, f32[2,2,64,128]{3,2,1,0:T(8,128)S(1)}, u32[]{:S(2)}, u32[]{:S(2)}) collective-permute-start(f32[2,2,64,128]{3,2,1,0:T(8,128)S(1)} %get-tuple-element.832), channel_id=1, source_target_pairs={{16,0},{32,16},{48,32},{64,48},{80,64},{96,80},{112,96},{17,1},{33... | collective-permute-start | bytes 393224 | tf_op jit(solution)/shard_map/while/body/eval_jaxpr/ppermute | solution.py:26
  460.7 15.7 %collective-permute-start.2 = (f32[2,2,256,64]{3,2,1,0:T(8,128)S(1)}, f32[2,2,256,64]{3,2,1,0:T(8,128)S(1)}, u32[]{:S(2)}, u32[]{:S(2)}) collective-permute-start(f32[2,2,256,64]{3,2,1,0:T(8,128)S(1)} %get-tuple-element.833), channel_id=1, source_target_pairs={{1,0},{2,1},{3,2},{4,3},{5,4},{6,5},{7,6},{8,7},{9,8},{10,9},{11,1... | collective-permute-start | bytes 786440 | tf_op jit(solution)/shard_map/while/body/eval_jaxpr/ppermute | solution.py:26
  465.4 12.6 %collective-permute-start.3 = (f32[2,2,256,64]{3,2,1,0:T(8,128)S(1)}, f32[2,2,256,64]{3,2,1,0:T(8,128)S(1)}, u32[]{:S(2)}, u32[]{:S(2)}) collective-permute-start(f32[2,2,256,64]{3,2,1,0:T(8,128)S(1)} %get-tuple-element.834), channel_id=1, source_target_pairs={{0,1},{1,2},{2,3},{3,4},{4,5},{5,6},{6,7},{7,8},{8,9},{9,10},{10,1... | collective-permute-start | bytes 786440 | tf_op jit(solution)/shard_map/while/body/eval_jaxpr/ppermute | solution.py:25
  523.1 12.4 %collective-permute-start.4 = (f32[2,2,64,256]{3,2,1,0:T(8,128)S(1)}, f32[2,2,64,256]{3,2,1,0:T(8,128)S(1)}, u32[]{:S(2)}, u32[]{:S(2)}) collective-permute-start(f32[2,2,64,256]{3,2,1,0:T(8,128)S(1)} %slice.373), channel_id=1, source_target_pairs={{0,16},{16,32},{32,48},{48,64},{64,80},{80,96},{96,112},{1,17},{17... | collective-permute-start | bytes 786440 | tf_op jit(solution)/shard_map/while/body/eval_jaxpr/ppermute | solution.py:15
  535.6 8.3 %collective-permute-start.5 = (f32[2,2,64,256]{3,2,1,0:T(8,128)S(1)}, f32[2,2,64,256]{3,2,1,0:T(8,128)S(1)}, u32[]{:S(2)}, u32[]{:S(2)}) collective-permute-start(f32[2,2,64,256]{3,2,1,0:T(8,128)S(1)} %get-tuple-element.858), channel_id=1, source_target_pairs={{16,0},{32,16},{48,32},{64,48},{80,64},{96,80},{112,96},{17,1},{33... | collective-permute-start | bytes 786440 | tf_op jit(solution)/shard_map/while/body/eval_jaxpr/ppermute | solution.py:15
  544.0 9.8 %collective-permute-start.6 = (f32[2,2,128,64]{3,2,1,0:T(8,128)S(1)}, f32[2,2,128,64]{3,2,1,0:T(8,128)S(1)}, u32[]{:S(2)}, u32[]{:S(2)}) collective-permute-start(f32[2,2,128,64]{3,2,1,0:T(8,128)S(1)} %fusion.646), channel_id=1, source_target_pairs={{0,1},{1,2},{2,3},{3,4},{4,5},{5,6},{6,7},{7,8},{8,9},{9,10},{10,1... | collective-permute-start | bytes 393224 | tf_op jit(solution)/shard_map/while/body/eval_jaxpr/ppermute | solution.py:15
  554.0 5.8 collective-permute-start.7
  560.0 10.5 %collective-permute-start = (f32[2,2,64,128]{3,2,1,0:T(8,128)S(1)}, f32[2,2,64,128]{3,2,1,0:T(8,128)S(1)}, u32[]{:S(2)}, u32[]{:S(2)}) collective-permute-start(f32[2,2,64,128]{3,2,1,0:T(8,128)S(1)} %get-tuple-element.831), channel_id=1, source_target_pairs={{0,16},{16,32},{32,48},{48,64},{64,80},{80,96},{96,112},{1,17},{17... | collective-permute-start | bytes 393224 | tf_op jit(solution)/shard_map/while/body/eval_jaxpr/ppermute | solution.py:25
  562.0 10.0 %collective-permute-start.1 = (f32[2,2,64,128]{3,2,1,0:T(8,128)S(1)}, f32[2,2,64,128]{3,2,1,0:T(8,128)S(1)}, u32[]{:S(2)}, u32[]{:S(2)}) collective-permute-start(f32[2,2,64,128]{3,2,1,0:T(8,128)S(1)} %get-tuple-element.832), channel_id=1, source_target_pairs={{16,0},{32,16},{48,32},{64,48},{80,64},{96,80},{112,96},{17,1},{33... | collective-permute-start | bytes 393224 | tf_op jit(solution)/shard_map/while/body/eval_jaxpr/ppermute | solution.py:26
  572.2 15.7 %collective-permute-start.2 = (f32[2,2,256,64]{3,2,1,0:T(8,128)S(1)}, f32[2,2,256,64]{3,2,1,0:T(8,128)S(1)}, u32[]{:S(2)}, u32[]{:S(2)}) collective-permute-start(f32[2,2,256,64]{3,2,1,0:T(8,128)S(1)} %get-tuple-element.833), channel_id=1, source_target_pairs={{1,0},{2,1},{3,2},{4,3},{5,4},{6,5},{7,6},{8,7},{9,8},{10,9},{11,1... | collective-permute-start | bytes 786440 | tf_op jit(solution)/shard_map/while/body/eval_jaxpr/ppermute | solution.py:26
  577.0 12.6 %collective-permute-start.3 = (f32[2,2,256,64]{3,2,1,0:T(8,128)S(1)}, f32[2,2,256,64]{3,2,1,0:T(8,128)S(1)}, u32[]{:S(2)}, u32[]{:S(2)}) collective-permute-start(f32[2,2,256,64]{3,2,1,0:T(8,128)S(1)} %get-tuple-element.834), channel_id=1, source_target_pairs={{0,1},{1,2},{2,3},{3,4},{4,5},{5,6},{6,7},{7,8},{8,9},{9,10},{10,1... | collective-permute-start | bytes 786440 | tf_op jit(solution)/shard_map/while/body/eval_jaxpr/ppermute | solution.py:25
  634.6 12.4 %collective-permute-start.4 = (f32[2,2,64,256]{3,2,1,0:T(8,128)S(1)}, f32[2,2,64,256]{3,2,1,0:T(8,128)S(1)}, u32[]{:S(2)}, u32[]{:S(2)}) collective-permute-start(f32[2,2,64,256]{3,2,1,0:T(8,128)S(1)} %slice.373), channel_id=1, source_target_pairs={{0,16},{16,32},{32,48},{48,64},{64,80},{80,96},{96,112},{1,17},{17... | collective-permute-start | bytes 786440 | tf_op jit(solution)/shard_map/while/body/eval_jaxpr/ppermute | solution.py:15
  647.1 8.3 %collective-permute-start.5 = (f32[2,2,64,256]{3,2,1,0:T(8,128)S(1)}, f32[2,2,64,256]{3,2,1,0:T(8,128)S(1)}, u32[]{:S(2)}, u32[]{:S(2)}) collective-permute-start(f32[2,2,64,256]{3,2,1,0:T(8,128)S(1)} %get-tuple-element.858), channel_id=1, source_target_pairs={{16,0},{32,16},{48,32},{64,48},{80,64},{96,80},{112,96},{17,1},{33... | collective-permute-start | bytes 786440 | tf_op jit(solution)/shard_map/while/body/eval_jaxpr/ppermute | solution.py:15
  655.5 9.8 %collective-permute-start.6 = (f32[2,2,128,64]{3,2,1,0:T(8,128)S(1)}, f32[2,2,128,64]{3,2,1,0:T(8,128)S(1)}, u32[]{:S(2)}, u32[]{:S(2)}) collective-permute-start(f32[2,2,128,64]{3,2,1,0:T(8,128)S(1)} %fusion.646), channel_id=1, source_target_pairs={{0,1},{1,2},{2,3},{3,4},{4,5},{5,6},{6,7},{7,8},{8,9},{9,10},{10,1... | collective-permute-start | bytes 393224 | tf_op jit(solution)/shard_map/while/body/eval_jaxpr/ppermute | solution.py:15
  665.5 5.8 collective-permute-start.7
  (5 other events, 4.2 us)
where the time goes:
time: 677 us; the launch traced here: 672 us
  waiting for transfers between devices  185 us (27%)
  matrix products  165 us (24%)
  starting transfers between devices  153 us (23%)
  loops' own time  95.7 us (14%)
  local copies, waits for them, and re-layouts  59.1 us (9%)
  other arithmetic  13.3 us (2%)
    ppermute x24, waiting for transfers between devices, shifted(): return lax.ppermute(block, axis, route)  160 us
    dot_general x144, matrix products, right_mul(): jnp.einsum('...ij,jk->...ik', field, matrix, precision=lax.Precision.HIGH...  85.4 us
    dot_general x144, matrix products, left_mul(): jnp.einsum('ij,...jk->...ik', matrix, field, precision=lax.Precision.HIGH...  80 us
    ppermute x12, starting transfers between devices, with_halo(): after = lax.ppermute(initial, axis, down)  70.3 us
    ppermute x24, starting transfers between devices, shifted(): return lax.ppermute(block, axis, route)  58.1 us
    another operation x1, loops' own time, local(): return lax.fori_loop(0, NB, period_step, object_field)  48.4 us
    another operation x6, loops' own time, period_step(): total = lax.fori_loop(0, batch, add_piece, jnp.zeros_like(padded))  47.2 us
    dynamic_update_slice x12, local copies, waits for them, and re-layouts, add_piece(): return lax.dynamic_update_slice(total, current + grads[member], place)  39.8 us
  transfers between devices with their start and end apart: 48, of which 42 were waited for; matrix products, arithmetic and copies ran while one was open for 1% of the time, Pallas kernels for 0%

commit v1 on v0

v1 whole, which is shorter than its diff:
```python
import math

import jax
import jax.numpy as jnp
import ml_dtypes
import numpy as np
from jax import lax
from jax.experimental import pallas as pl
from jax.experimental.pallas import tpu as pltpu
from jax.sharding import PartitionSpec as P

MESH = pl.DeviceIdType.MESH
N = 128
H = 64
BATCH = 2
NB = 6
STEP = 0.08
F32 = jnp.float32
BF16 = jnp.bfloat16

Y_RE, Z_IM, M_RS, Z_M, Z_RE, Y_IM = range(6)
K_YRE, K_ZIM_U, K_ZIM_D, K_M, K_ZM_U, K_ZM_D, K_ZRE_U, K_ZRE_D, K_YIM, K_P3 = range(10)
TOP = pl.ds(0, N)
BOT = pl.ds(N, N)


def dft_tables():
    index = np.arange(N)
    phase = (index[:, None] * index[None, :] % N) * (2.0 * math.pi / N)
    c, s = np.cos(phase) / math.sqrt(N), np.sin(phase) / math.sqrt(N)
    rights, lefts = [], []
    for sign in (-1.0, 1.0):
        right = np.block([[c, sign * s], [-sign * s, c]])
        left = right.T
        for m, out, axis in ((right, rights, 0), (left, lefts, 1)):
            hi = m.astype(ml_dtypes.bfloat16)
            lo = (m - hi.astype(np.float64)).astype(ml_dtypes.bfloat16)
            out.append(np.concatenate([hi, hi, lo], axis=axis))
    return np.stack(rights), np.stack(lefts)


def cmul(ar, ai, br, bi):
    return ar * br - ai * bi, ar * bi + ai * br


def kernel(offs, cnt, obj, probe, prop, inten, wr, wl, out, o0, o1, d, z, r, a, q, psi, pat, ssem, rsem):
    objects = (o0, o1)
    gx = lax.axis_index("gx")
    gy = lax.axis_index("gy")
    core = lax.rem(gy, 2)
    has_u = gx > 0
    has_d = gx < 7
    has_o = jnp.logical_and(gy > 0, gy < 15)
    up = (jnp.maximum(gx - 1, 0), gy)
    dn = (jnp.minimum(gx + 1, 7), gy)
    mate = (gx, gy + 1 - 2 * core)
    outer = (gx, jnp.clip(gy - 1 + 2 * core, 0, 15))
    hl = 1 - core
    hr = core

    lane = lax.broadcasted_iota(jnp.int32, (1, N), 1)
    row = lax.broadcasted_iota(jnp.int32, (2 * N, N), 0)
    row_ok = jnp.logical_and(row >= jnp.where(gx == 0, H, 0), row < jnp.where(gx == 7, 3 * H, 4 * H))
    l_ok = lane >= jnp.where(gy == 0, H, 0)
    r_ok = lane < jnp.where(gy == 15, H, N)

    def desc(kind, src, dst, s, slot, dev):
        return pltpu.make_async_remote_copy(
            src_ref=src,
            dst_ref=dst,
            send_sem=ssem.at[kind, s, slot],
            recv_sem=rsem.at[kind, s, slot],
            device_id=dev,
            device_id_type=MESH,
        )

    def copy(kind, s, slot):
        if kind == K_YRE:
            return desc(kind, d.at[s, 1, 0], r.at[Y_RE, s, slot], s, slot, outer)
        if kind == K_ZIM_U:
            return desc(kind, d.at[s, 1, 1, TOP], r.at[Z_IM, s, slot, BOT], s, slot, up)
        if kind == K_ZIM_D:
            return desc(kind, d.at[s, 1, 1, BOT], r.at[Z_IM, s, slot, TOP], s, slot, dn)
        if kind == K_M:
            return desc(kind, d.at[s, 0, 1 - core], r.at[M_RS, s, slot], s, slot, mate)
        if kind == K_ZM_U:
            return desc(kind, a.at[2, s, TOP], r.at[Z_M, s, slot, BOT], s, slot, up)
        if kind == K_ZM_D:
            return desc(kind, a.at[2, s, BOT], r.at[Z_M, s, slot, TOP], s, slot, dn)
        if kind == K_ZRE_U:
            return desc(kind, a.at[0, s, TOP], r.at[Z_RE, s, slot, BOT], s, slot, up)
        if kind == K_ZRE_D:
            return desc(kind, a.at[0, s, BOT], r.at[Z_RE, s, slot, TOP], s, slot, dn)
        if kind == K_YIM:
            return desc(kind, a.at[1, s], r.at[Y_IM, s, slot], s, slot, outer)
        return desc(kind, objects[s].at[0, core], objects[s].at[0, core], s, slot, mate)

    senders = {
        K_YRE: has_o, K_ZIM_U: has_u, K_ZIM_D: has_d, K_M: None, K_ZM_U: has_u, K_ZM_D: has_d,
        K_ZRE_U: has_u, K_ZRE_D: has_d, K_YIM: has_o, K_P3: None,
    }
    receivers = dict(senders)
    for ku, kd in ((K_ZIM_U, K_ZIM_D), (K_ZM_U, K_ZM_D), (K_ZRE_U, K_ZRE_D)):
        receivers[ku], receivers[kd] = has_d, has_u

    def guarded(cond, fn):
        if cond is None:
            fn()
        else:
            pl.when(cond)(fn)

    def send(kind, s, slot):
        guarded(senders[kind], lambda: copy(kind, s, slot).start())

    def recv(kind, s, slot):
        if kind == K_P3:
            desc(kind, objects[s].at[0, core], objects[s].at[0, 1 - core], s, slot, mate).wait_recv()
        else:
            guarded(receivers[kind], lambda: copy(kind, s, slot).wait_recv())

    def sent(kind, s, slot):
        guarded(senders[kind], lambda: copy(kind, s, slot).wait_send())

    def start(s, slot):
        send(K_M, s, slot)
        send(K_YRE, s, slot)
        send(K_ZIM_U, s, slot)
        send(K_ZIM_D, s, slot)

    def mid_m(s, slot):
        recv(K_M, s, slot)
        a[2, s] = d[s, 0, core] + r[M_RS, s, slot]
        send(K_ZM_U, s, slot)
        send(K_ZM_D, s, slot)

    def mid_re(s, slot):
        recv(K_YRE, s, slot)
        a[0, s] = d[s, 1, 0] + r[Y_RE, s, slot]
        send(K_ZRE_U, s, slot)
        send(K_ZRE_D, s, slot)

    def mid_im(s, slot):
        recv(K_ZIM_U, s, slot)
        recv(K_ZIM_D, s, slot)
        a[1, s] = d[s, 1, 1] + r[Z_IM, s, slot]
        send(K_YIM, s, slot)

    def mid_back(s, slot):
        recv(K_ZM_U, s, slot)
        recv(K_ZM_D, s, slot)
        objects[s][0, core] = objects[s][0, core] + (a[2, s] + r[Z_M, s, slot])
        send(K_P3, s, slot)

    def finish(s, slot):
        recv(K_ZRE_U, s, slot)
        recv(K_ZRE_D, s, slot)
        objects[s][1, 0] = objects[s][1, 0] + (a[0, s] + r[Z_RE, s, slot])
        recv(K_YIM, s, slot)
        objects[s][1, 1] = objects[s][1, 1] + (a[1, s] + r[Y_IM, s, slot])
        recv(K_P3, s, slot)
        for kind in range(10):
            sent(kind, s, slot)

    def exchange(slot):
        mid_m(1, slot)
        mid_m(0, slot)
        mid_re(1, slot)
        mid_im(1, slot)
        mid_re(0, slot)
        mid_im(0, slot)
        mid_back(0, slot)
        mid_back(1, slot)
        finish(0, slot)

    r[...] = jnp.zeros_like(r)
    for o in objects:
        o[...] = jnp.zeros_like(o)
    d[...] = jnp.zeros_like(d)
    z[...] = jnp.zeros_like(z)
    barrier = pltpu.get_barrier_semaphore()
    for cond, dev in ((None, mate), (has_u, up), (has_d, dn), (has_o, outer)):
        guarded(cond, lambda dev=dev: pl.semaphore_signal(barrier, inc=1, device_id=dev, device_id_type=MESH))
    count = 1 + has_u.astype(jnp.int32) + has_d.astype(jnp.int32) + has_o.astype(jnp.int32)
    pl.semaphore_wait(barrier, count)

    for s in (1, 0):
        for c in range(2):
            tile = pltpu.roll(obj[s, c], H, 1)
            d[s, hl, c, pl.ds(H, N)] = jnp.where(lane >= H, tile, 0.0)
            d[s, hr, c, pl.ds(H, N)] = jnp.where(lane < H, tile, 0.0)
        start(s, 0)
    q[0] = jnp.cos(prop[...])
    q[1] = jnp.sin(prop[...])
    exchange(0)

    def split(x):
        hi = x.astype(BF16)
        return hi, (x - hi.astype(F32)).astype(BF16)

    def transform(re, im, inverse):
        x = jnp.concatenate([jnp.concatenate([re[m], im[m]], 1) for m in range(BATCH)], 0)
        hi, lo = split(x)
        y = jnp.dot(jnp.concatenate([hi, lo, hi], 1), wr[inverse], preferred_element_type=F32)
        x = jnp.concatenate(
            [jnp.concatenate([y[:N, :N], y[N:, :N]], 1), jnp.concatenate([y[:N, N:], y[N:, N:]], 1)], 0
        )
        hi, lo = split(x)
        y = jnp.dot(wl[inverse], jnp.concatenate([hi, lo, hi], 0), preferred_element_type=F32)
        return (y[:N, :N], y[:N, N:]), (y[N:, :N], y[N:, N:])

    def patch(s, c, r0, q0):
        left = objects[s][hl, c, pl.ds(r0, N), :]
        right = objects[s][hr, c, pl.ds(r0, N), :]
        return pltpu.roll(jnp.where(lane >= q0, left, right), (N - q0) & (N - 1), 1)

    def scatter(s, places, grads):
        for m in range(BATCH):
            r0, q0, weight = places[m]
            fl = jnp.where(jnp.logical_and(lane >= q0, l_ok), weight, 0.0)
            fr = jnp.where(jnp.logical_and(lane < q0, r_ok), weight, 0.0)
            for c in range(2):
                g = pltpu.roll(grads[c][m], q0 & (N - 1), 1)
                z[m, 0, c, pl.ds(N, N)] = g * fl
                z[m, 1, c, pl.ds(N, N)] = g * fr
        for h, half in ((0, hl), (1, hr)):
            for c in range(2):
                total = z[0, h, c, pl.ds(N - places[0][0], 2 * N), :] + z[1, h, c, pl.ds(N - places[1][0], 2 * N), :]
                d[s, half, c] = jnp.where(row_ok, total, 0.0)

    def batch(b, carry):
        slot = lax.rem(b + 1, 2)
        before = lax.rem(b, 2)
        places = []
        for m in range(BATCH):
            n = b * BATCH + m
            weight = jnp.where(n < cnt[0, 0], -STEP, 0.0).astype(F32)
            places.append((offs[n, 0], offs[n, 1], weight))
        pr, pi = probe[0], probe[1]
        re, im = [], []
        for m in range(BATCH):
            r0, q0, _ = places[m]
            x, y = cmul(pr, pi, patch(0, 0, r0, q0), patch(0, 1, r0, q0))
            re.append(x)
            im.append(y)
        re, im = transform(re, im, 0)
        both = [cmul(re[m], im[m], q[0], q[1]) for m in range(BATCH)]
        re, im = transform([x for x, _ in both], [y for _, y in both], 1)
        for m in range(BATCH):
            psi[m, 0] = re[m]
            psi[m, 1] = im[m]
        finish(1, before)
        both = []
        for m in range(BATCH):
            r0, q0, _ = places[m]
            for c in range(2):
                pat[m, c] = patch(1, c, r0, q0)
            both.append(cmul(psi[m, 0], psi[m, 1], pat[m, 0], pat[m, 1]))
        re, im = transform([x for x, _ in both], [y for _, y in both], 0)
        excess = [re[m] * re[m] + im[m] * im[m] - inten[b * BATCH + m] for m in range(BATCH)]
        re, im = transform([excess[m] * re[m] for m in range(BATCH)], [excess[m] * im[m] for m in range(BATCH)], 1)
        both = [cmul(psi[m, 0], -psi[m, 1], re[m], im[m]) for m in range(BATCH)]
        scatter(1, places, ([x for x, _ in both], [y for _, y in both]))
        start(1, slot)
        both = [cmul(pat[m, 0], -pat[m, 1], re[m], im[m]) for m in range(BATCH)]
        re, im = transform([x for x, _ in both], [y for _, y in both], 0)
        both = [cmul(re[m], im[m], q[0], -q[1]) for m in range(BATCH)]
        re, im = transform([x for x, _ in both], [y for _, y in both], 1)
        both = [cmul(re[m], im[m], pr, -pi) for m in range(BATCH)]
        scatter(0, places, ([x for x, _ in both], [y for _, y in both]))
        start(0, slot)
        exchange(slot)
        return carry

    lax.fori_loop(0, NB, batch, 0)
    finish(1, NB % 2)
    for s in range(2):
        for c in range(2):
            left = objects[s][hl, c, pl.ds(H, N), :]
            right = objects[s][hr, c, pl.ds(H, N), :]
            out[s, c] = pltpu.roll(jnp.where(lane >= H, left, right), H, 1)


def solution(mesh):
    rights, lefts = dft_tables()

    def local(object_field, probe, propagator, offsets, counts, intensity):
        vmem = pl.BlockSpec(memory_space=pltpu.VMEM)
        smem = pl.BlockSpec(memory_space=pltpu.SMEM)
        return pl.pallas_call(
            kernel,
            out_shape=jax.ShapeDtypeStruct((2, 2, N, N), F32),
            in_specs=[smem, smem] + [vmem] * 6,
            out_specs=vmem,
            scratch_shapes=[
                pltpu.VMEM((2, 2, 2 * N, N), F32),
                pltpu.VMEM((2, 2, 2 * N, N), F32),
                pltpu.VMEM((2, 2, 2, 2 * N, N), F32),
                pltpu.VMEM((BATCH, 2, 2, 3 * N, N), F32),
                pltpu.VMEM((6, 2, 2, 2 * N, N), F32),
                pltpu.VMEM((3, 2, 2 * N, N), F32),
                pltpu.VMEM((2, N, N), F32),
                pltpu.VMEM((BATCH, 2, N, N), F32),
                pltpu.VMEM((BATCH, 2, N, N), F32),
                pltpu.SemaphoreType.DMA((10, 2, 2)),
                pltpu.SemaphoreType.DMA((10, 2, 2)),
            ],
            compiler_params=pltpu.CompilerParams(
                collective_id=0, has_side_effects=True, vmem_limit_bytes=48 * 1024 * 1024
            ),
        )(
            offsets[0, 0], counts, object_field, probe, propagator, intensity[0, 0],
            jnp.asarray(rights), jnp.asarray(lefts),
        )

    in_specs = (
        P(None, None, "gx", "gy"),
        P(),
        P(),
        P("gx", "gy", None, None),
        P("gx", "gy"),
        P("gx", "gy", None, None, None),
    )
    out_specs = P(None, None, "gx", "gy")
    return jax.shard_map(local, mesh=mesh, in_specs=in_specs, out_specs=out_specs, check_vma=False)
```

time: 677 us -> 147 us (0.22)
  waiting for transfers between devices: 185 us -> 0 us
  matrix products: 165 us -> 0 us
  starting transfers between devices: 153 us -> 0 us
  Pallas kernels: 0 us -> 138 us
  loops' own time: 95.7 us -> 0 us
  local copies, waits for them, and re-layouts: 59.1 us -> 7.56 us
  other arithmetic: 13.3 us -> 0 us
    ppermute x48 -> x0, waiting for transfers between devices: 185 us -> none  [the longest x24 160 us: shifted(): return lax.ppermute(block, axis, route)]
    dot_general x288 -> x0, matrix products: 165 us -> none  [the longest x144 85.4 us: right_mul(): jnp.einsum('...ij,jk->...ik', field, matrix, precision=lax.Precision.HIGH...]
    ppermute x48 -> x0, starting transfers between devices: 153 us -> none  [the longest x12 70.3 us: with_halo(): after = lax.ppermute(initial, axis, down)]
    pallas_call x0 -> x1, Pallas kernels: none -> 138 us  [local(): pl.pallas_call(kernel, out_shape=jax.ShapeDtypeStruct((2, 2, N, N), F32),...]
    another operation x7 -> x0, loops' own time: 95.7 us -> none  [the longest x1 48.4 us: local(): return lax.fori_loop(0, NB, period_step, object_field)]
    dynamic_update_slice x12 -> x0, local copies, waits for them, and re-layouts: 39.8 us -> none  [add_piece(): return lax.dynamic_update_slice(total, current + grads[member], place)]
    dynamic_slice x24 -> x0, local copies, waits for them, and re-layouts: 8.49 us -> none  [the longest x12 7.46 us: add_piece(): place = (zero, zero, slot_offsets[member, 0], slot_offsets[member, 1])]
  transfers between devices with their start and end apart: 48 -> 0, of which waited for: 42 -> 0; matrix products, arithmetic and copies ran while one was open for 1% -> 0% of each run, Pallas kernels for 0% -> 0%
where the time goes in v1:
time: 147 us; the launch traced here: 146 us
  Pallas kernels  138 us (94%)
  local copies, waits for them, and re-layouts  7.56 us (5%)
    pallas_call x1, Pallas kernels, local(): pl.pallas_call(kernel, out_shape=jax.ShapeDtypeStruct((2, 2, N, N), F32),...  138 us
    unnamed x15, local copies, waits for them, and re-layouts  7.47 us

profile of v1, /device:TPU:6, one launch (start us, length us, event | category | flops | bytes accessed | tf_op | source)
XLA Modules:
  0.0 146.4 jit_solution(9172889357400712094)
XLA Ops:
  0.7 0.0 copy-start.6
  0.7 0.7 copy-done.6
  1.3 0.1 copy.9.offs
  1.4 0.0 copy-start
  1.4 1.1 copy-done
  2.6 0.0 copy-start.1
  2.6 1.1 copy-done.1
  3.7 0.0 copy-start.2
  3.7 1.1 copy-done.2
  4.8 0.0 copy-start.3
  4.8 0.9 copy-done.3
  5.8 0.0 copy-start.4
  5.8 0.9 copy-done.4
  6.7 0.0 copy-start.5
  6.7 0.8 copy-done.5
  7.5 138.2 %shard_map.82 = f32[2,2,128,128]{3,2,1,0:T(8,128)S(1)} custom-call(s32[12,2]{1,0:T(8,128)S(1)} %copy.9.offs, s32[1,1]{1,0:T(1,128)S(6)} %copy.11.cnt, f32[2,2,128,128]{3,2,1,0:T(8,128)S(1)} %copy-done.3, f32[2,128,128]{2,1,0:T(8,128)S(1)} %copy-done.4, f32[128,128]{1,0:T(8,128)S(1)} %copy-done.5, f32[12,128,128]{2,1,0:T(8,128)S(1)} %bitcast.2, ...), custom_call_target="tpu_custom_call" | custom-call | tf_op jit(solution)/shard_map/pallas_call | solution.py:289
  145.7 0.7 copy.12
Async XLA Ops:
  0.7 0.7 copy-start.6
  1.4 1.1 copy-start
  2.6 1.1 copy-start.1
  3.7 1.1 copy-start.2
  4.8 0.9 copy-start.3
  5.8 0.9 copy-start.4
  6.7 0.8 copy-start.5

commit v2 on v1

--- a/solution.py
+++ b/solution.py
@@ -28,33 +28,61 @@
     index = np.arange(N)
     phase = (index[:, None] * index[None, :] % N) * (2.0 * math.pi / N)
     c, s = np.cos(phase) / math.sqrt(N), np.sin(phase) / math.sqrt(N)
-    rights, lefts = [], []
+    out = []
     for sign in (-1.0, 1.0):
-        right = np.block([[c, sign * s], [-sign * s, c]])
-        left = right.T
-        for m, out, axis in ((right, rights, 0), (left, lefts, 1)):
-            hi = m.astype(ml_dtypes.bfloat16)
-            lo = (m - hi.astype(np.float64)).astype(ml_dtypes.bfloat16)
-            out.append(np.concatenate([hi, hi, lo], axis=axis))
-    return np.stack(rights), np.stack(lefts)
+        m = np.block([[c, sign * s], [-sign * s, c]])
+        hi = m.astype(ml_dtypes.bfloat16)
+        out.append(np.stack([hi, (m - hi.astype(np.float64)).astype(ml_dtypes.bfloat16)]))
+    return np.stack(out)
+
+
+def place(hi_x, lo_x, y, z, core):
+    return hi_x * 4 + z, (lo_x * 4 + y) * 2 + core
+
+
+def parts(gx, gy):
+    return lax.div(gx, 4), lax.rem(gx, 4), lax.div(gy, 8), lax.rem(lax.div(gy, 2), 4), lax.rem(gy, 2)
+
+
+def tile_of(gx, gy):
+    hi_x, z, lo_x, y, core = parts(gx, gy)
+    lo_x = lax.rem(lo_x + hi_x, 2)
+    z = jnp.where(hi_x == 1, 3 - z, z)
+    y = jnp.where(lo_x == 1, 3 - y, y)
+    return place(hi_x, lo_x, y, z, core)
+
+
+def device_of(gx, gy):
+    hi_x, z, lo_x, y, core = parts(gx, gy)
+    z = jnp.where(hi_x == 1, 3 - z, z)
+    y = jnp.where(lo_x == 1, 3 - y, y)
+    return place(hi_x, lax.rem(lo_x + hi_x, 2), y, z, core)
 
 
 def cmul(ar, ai, br, bi):
     return ar * br - ai * bi, ar * bi + ai * br
 
 
-def kernel(offs, cnt, obj, probe, prop, inten, wr, wl, out, o0, o1, d, z, r, a, q, psi, pat, ssem, rsem):
+def kernel(
+    offs_in, cnt_in, obj, probe_in, prop_in, inten_in, w_in, out,
+    o0, o1, d, z, r, a, q, psi, pat, tile, inten, fin, probe, prop, w, offs, cnt,
+    ssem, rsem, in_send, in_recv, out_send, out_recv, lsem,
+):
     objects = (o0, o1)
-    gx = lax.axis_index("gx")
-    gy = lax.axis_index("gy")
+    me = (lax.axis_index("gx"), lax.axis_index("gy"))
+    gx, gy = tile_of(*me)
     core = lax.rem(gy, 2)
+    home = (gx, gy)
+    worker = device_of(*me)
+    moved = jnp.logical_or(gx != me[0], gy != me[1])
+    stays = jnp.logical_not(moved)
     has_u = gx > 0
     has_d = gx < 7
     has_o = jnp.logical_and(gy > 0, gy < 15)
-    up = (jnp.maximum(gx - 1, 0), gy)
-    dn = (jnp.minimum(gx + 1, 7), gy)
-    mate = (gx, gy + 1 - 2 * core)
-    outer = (gx, jnp.clip(gy - 1 + 2 * core, 0, 15))
+    up = device_of(jnp.maximum(gx - 1, 0), gy)
+    dn = device_of(jnp.minimum(gx + 1, 7), gy)
+    mate = device_of(gx, gy + 1 - 2 * core)
+    outer = device_of(gx, jnp.clip(gy - 1 + 2 * core, 0, 15))
     hl = 1 - core
     hr = core
 
@@ -172,23 +200,67 @@
         mid_back(1, slot)
         finish(0, slot)
 
+    inputs = [(offs_in, offs), (cnt_in, cnt)]
+    inputs += [(obj.at[s], tile.at[s]) for s in range(2)]
+
+    def pass_on(i, src, dst):
+        return pltpu.make_async_remote_copy(
+            src_ref=src,
+            dst_ref=dst,
+            send_sem=in_send.at[i],
+            recv_sem=in_recv.at[i],
+            device_id=worker,
+            device_id_type=MESH,
+        )
+
+    def keep(i, src, dst):
+        return pltpu.make_async_copy(src, dst, in_send.at[i])
+
+    def pass_start(i, src, dst):
+        pl.when(moved)(lambda: pass_on(i, src, dst).start())
+        pl.when(stays)(lambda: keep(i, src, dst).start())
+
+    def pass_wait(i, src, dst):
+        @pl.when(moved)
+        def _():
+            pass_on(i, src, dst).wait_send()
+            pass_on(i, src, dst).wait_recv()
+
+        pl.when(stays)(lambda: keep(i, src, dst).wait())
+
+    def frames(b):
+        return 4 + b, inten_in.at[pl.ds(BATCH * b, BATCH)], inten.at[pl.ds(BATCH * b, BATCH)]
+
+    consts = [(probe_in, probe), (prop_in, prop), (w_in, w)]
+    for i, (src, dst) in enumerate(consts):
+        pltpu.make_async_copy(src, dst, lsem.at[i]).start()
+
+    barrier = pltpu.get_barrier_semaphore()
+    greet = ((None, mate), (has_u, up), (has_d, dn), (has_o, outer), (moved, home), (moved, worker))
     r[...] = jnp.zeros_like(r)
     for o in objects:
         o[...] = jnp.zeros_like(o)
     d[...] = jnp.zeros_like(d)
     z[...] = jnp.zeros_like(z)
-    barrier = pltpu.get_barrier_semaphore()
-    for cond, dev in ((None, mate), (has_u, up), (has_d, dn), (has_o, outer)):
+    for cond, dev in greet:
         guarded(cond, lambda dev=dev: pl.semaphore_signal(barrier, inc=1, device_id=dev, device_id_type=MESH))
-    count = 1 + has_u.astype(jnp.int32) + has_d.astype(jnp.int32) + has_o.astype(jnp.int32)
+    count = 1 + sum(jnp.where(cond, 1, 0) for cond, _ in greet[1:])
     pl.semaphore_wait(barrier, count)
-
-    for s in (1, 0):
+    for i in range(4):
+        pass_start(i, *inputs[i])
+    pass_start(*frames(0))
+
+    for s in (0, 1):
+        pass_wait(2 + s, *inputs[2 + s])
         for c in range(2):
-            tile = pltpu.roll(obj[s, c], H, 1)
-            d[s, hl, c, pl.ds(H, N)] = jnp.where(lane >= H, tile, 0.0)
-            d[s, hr, c, pl.ds(H, N)] = jnp.where(lane < H, tile, 0.0)
+            cells = pltpu.roll(tile[s, c], H, 1)
+            d[s, hl, c, pl.ds(H, N)] = jnp.where(lane >= H, cells, 0.0)
+            d[s, hr, c, pl.ds(H, N)] = jnp.where(lane < H, cells, 0.0)
         start(s, 0)
+    for i, (src, dst) in enumerate(consts):
+        pltpu.make_async_copy(src, dst, lsem.at[i]).wait()
+    for i in range(2):
+        pass_wait(i, *inputs[i])
     q[0] = jnp.cos(prop[...])
     q[1] = jnp.sin(prop[...])
     exchange(0)
@@ -200,12 +272,14 @@
     def transform(re, im, inverse):
         x = jnp.concatenate([jnp.concatenate([re[m], im[m]], 1) for m in range(BATCH)], 0)
         hi, lo = split(x)
-        y = jnp.dot(jnp.concatenate([hi, lo, hi], 1), wr[inverse], preferred_element_type=F32)
+        right = jnp.concatenate([w[inverse, 0], w[inverse, 0], w[inverse, 1]], 0)
+        y = jnp.dot(jnp.concatenate([hi, lo, hi], 1), right, preferred_element_type=F32)
         x = jnp.concatenate(
             [jnp.concatenate([y[:N, :N], y[N:, :N]], 1), jnp.concatenate([y[:N, N:], y[N:, N:]], 1)], 0
         )
         hi, lo = split(x)
-        y = jnp.dot(wl[inverse], jnp.concatenate([hi, lo, hi], 0), preferred_element_type=F32)
+        left = jnp.concatenate([w[1 - inverse, 0], w[1 - inverse, 0], w[1 - inverse, 1]], 1)
+        y = jnp.dot(left, jnp.concatenate([hi, lo, hi], 0), preferred_element_type=F32)
         return (y[:N, :N], y[:N, N:]), (y[N:, :N], y[N:, N:])
 
     def patch(s, c, r0, q0):
@@ -230,11 +304,12 @@
     def batch(b, carry):
         slot = lax.rem(b + 1, 2)
         before = lax.rem(b, 2)
+        pl.when(b < NB - 1)(lambda: pass_start(*frames(b + 1)))
         places = []
         for m in range(BATCH):
             n = b * BATCH + m
             weight = jnp.where(n < cnt[0, 0], -STEP, 0.0).astype(F32)
-            places.append((offs[n, 0], offs[n, 1], weight))
+            places.append((offs[0, n], offs[1, n], weight))
         pr, pi = probe[0], probe[1]
         re, im = [], []
         for m in range(BATCH):
@@ -256,6 +331,7 @@
                 pat[m, c] = patch(1, c, r0, q0)
             both.append(cmul(psi[m, 0], psi[m, 1], pat[m, 0], pat[m, 1]))
         re, im = transform([x for x, _ in both], [y for _, y in both], 0)
+        pass_wait(*frames(b))
         excess = [re[m] * re[m] + im[m] * im[m] - inten[b * BATCH + m] for m in range(BATCH)]
         re, im = transform([excess[m] * re[m] for m in range(BATCH)], [excess[m] * im[m] for m in range(BATCH)], 1)
         both = [cmul(psi[m, 0], -psi[m, 1], re[m], im[m]) for m in range(BATCH)]
@@ -271,26 +347,48 @@
         exchange(slot)
         return carry
 
-    lax.fori_loop(0, NB, batch, 0)
-    finish(1, NB % 2)
-    for s in range(2):
+    def send_home(s):
+        return pltpu.make_async_remote_copy(
+            src_ref=fin.at[s],
+            dst_ref=out.at[s],
+            send_sem=out_send.at[s],
+            recv_sem=out_recv.at[s],
+            device_id=home,
+            device_id_type=MESH,
+        )
+
+    def give(s):
         for c in range(2):
             left = objects[s][hl, c, pl.ds(H, N), :]
             right = objects[s][hr, c, pl.ds(H, N), :]
-            out[s, c] = pltpu.roll(jnp.where(lane >= H, left, right), H, 1)
+            fin[s, c] = pltpu.roll(jnp.where(lane >= H, left, right), H, 1)
+        pl.when(moved)(lambda: send_home(s).start())
+
+        @pl.when(stays)
+        def _():
+            out[s] = fin[s]
+
+    lax.fori_loop(0, NB, batch, 0)
+    give(0)
+    finish(1, NB % 2)
+    give(1)
+    for s in range(2):
+        @pl.when(moved)
+        def _():
+            send_home(s).wait_send()
+            send_home(s).wait_recv()
 
 
 def solution(mesh):
-    rights, lefts = dft_tables()
+    tables = dft_tables()
 
     def local(object_field, probe, propagator, offsets, counts, intensity):
-        vmem = pl.BlockSpec(memory_space=pltpu.VMEM)
-        smem = pl.BlockSpec(memory_space=pltpu.SMEM)
+        hbm = pl.BlockSpec(memory_space=pltpu.HBM)
         return pl.pallas_call(
             kernel,
             out_shape=jax.ShapeDtypeStruct((2, 2, N, N), F32),
-            in_specs=[smem, smem] + [vmem] * 6,
-            out_specs=vmem,
+            in_specs=[hbm] * 7,
+            out_specs=pl.BlockSpec(memory_space=pltpu.VMEM),
             scratch_shapes=[
                 pltpu.VMEM((2, 2, 2 * N, N), F32),
                 pltpu.VMEM((2, 2, 2 * N, N), F32),
@@ -301,15 +399,27 @@
                 pltpu.VMEM((2, N, N), F32),
                 pltpu.VMEM((BATCH, 2, N, N), F32),
                 pltpu.VMEM((BATCH, 2, N, N), F32),
+                pltpu.VMEM((2, 2, N, N), F32),
+                pltpu.VMEM((NB * BATCH, N, N), F32),
+                pltpu.VMEM((2, 2, N, N), F32),
+                pltpu.VMEM((2, N, N), F32),
+                pltpu.VMEM((N, N), F32),
+                pltpu.VMEM((2, 2, 2 * N, 2 * N), BF16),
+                pltpu.SMEM((2, NB * BATCH), jnp.int32),
+                pltpu.SMEM((1, 1), jnp.int32),
                 pltpu.SemaphoreType.DMA((10, 2, 2)),
                 pltpu.SemaphoreType.DMA((10, 2, 2)),
+                pltpu.SemaphoreType.DMA((4 + NB,)),
+                pltpu.SemaphoreType.DMA((4 + NB,)),
+                pltpu.SemaphoreType.DMA((2,)),
+                pltpu.SemaphoreType.DMA((2,)),
+                pltpu.SemaphoreType.DMA((3,)),
             ],
             compiler_params=pltpu.CompilerParams(
                 collective_id=0, has_side_effects=True, vmem_limit_bytes=48 * 1024 * 1024
             ),
         )(
-            offsets[0, 0], counts, object_field, probe, propagator, intensity[0, 0],
-            jnp.asarray(rights), jnp.asarray(lefts),
+            offsets[0, 0].T, counts, object_field, probe, propagator, intensity[0, 0], jnp.asarray(tables),
         )
 
     in_specs = (

time: 147 us -> 127 us (0.86)
  Pallas kernels: 138 us -> 119 us
    pallas_call x1, Pallas kernels: 138 us -> 119 us  [local(): pl.pallas_call(kernel, out_shape=jax.ShapeDtypeStruct((2, 2, N, N), F32),...]
    unnamed x15 -> x13, local copies, waits for them, and re-layouts: 7.47 us -> 6.24 us
where the time goes in v2:
time: 127 us; the launch traced here: 126 us
  Pallas kernels  119 us (94%)
  local copies, waits for them, and re-layouts  6.24 us (5%)
    pallas_call x1, Pallas kernels, local(): pl.pallas_call(kernel, out_shape=jax.ShapeDtypeStruct((2, 2, N, N), F32),...  119 us
    unnamed x13, local copies, waits for them, and re-layouts  6.24 us

profile of v2, /device:TPU:6, one launch (start us, length us, event | category | flops | bytes accessed | tf_op | source)
XLA Modules:
  0.0 126.4 jit_solution(12904523006619383015)
XLA Ops:
  0.7 0.0 copy-start.5
  0.7 0.7 copy-done.5
  1.3 0.0 copy-start
  1.3 1.1 copy-done
  2.5 0.0 copy-start.1
  2.5 1.0 copy-done.1
  3.5 0.0 copy-start.2
  3.5 0.9 copy-done.2
  4.5 0.0 copy-start.3
  4.5 0.9 copy-done.3
  5.4 0.0 copy-start.4
  5.4 0.8 copy-done.4
  6.2 119.5 %shard_map.73 = f32[2,2,128,128]{3,2,1,0:T(8,128)S(1)} custom-call(s32[2,12]{1,0:T(2,128)S(1)} %bitcast.5, s32[1,1]{1,0:T(1,128)S(6)} %copy.9.cnt_in, f32[2,2,128,128]{3,2,1,0:T(8,128)S(1)} %copy-done.2, f32[2,128,128]{2,1,0:T(8,128)S(1)} %copy-done.3, f32[128,128]{1,0:T(8,128)S(1)} %copy-done.4, f32[12,128,128]{2,1,0:T(8,128)S(1)} %bitcast.4, ...), custom_call_target="tpu_custom_call" | custom-call | tf_op jit(solution)/shard_map/pallas_call | solution.py:387
  125.7 0.7 copy.10
Async XLA Ops:
  0.7 0.7 copy-start.5
  1.3 1.1 copy-start
  2.5 1.0 copy-start.1
  3.5 0.9 copy-start.2
  4.5 0.9 copy-start.3
  5.4 0.8 copy-start.4

commit v3 on v2

--- a/solution.py
+++ b/solution.py
@@ -20,6 +20,8 @@
 
 Y_RE, Z_IM, M_RS, Z_M, Z_RE, Y_IM = range(6)
 K_YRE, K_ZIM_U, K_ZIM_D, K_M, K_ZM_U, K_ZM_D, K_ZRE_U, K_ZRE_D, K_YIM, K_P3 = range(10)
+FIRST, USUAL, LAST = range(3)
+ALL = pl.ds(0, 2 * N)
 TOP = pl.ds(0, N)
 BOT = pl.ds(N, N)
 
@@ -102,34 +104,61 @@
             device_id_type=MESH,
         )
 
-    def copy(kind, s, slot):
+    def up_rows(mode):
+        return {FIRST: (pl.ds(H, H), pl.ds(3 * H, H)), USUAL: (TOP, BOT), LAST: (pl.ds(0, H), pl.ds(N, H))}[mode]
+
+    def down_rows(mode):
+        return {FIRST: (pl.ds(N, H), pl.ds(0, H)), USUAL: (BOT, TOP), LAST: (pl.ds(3 * H, H), pl.ds(H, H))}[mode]
+
+    def first_rows(mode):
+        return pl.ds(H, N) if mode == FIRST else ALL
+
+    def last_rows(mode):
+        return pl.ds(H, N) if mode == LAST else ALL
+
+    def along_z(kind, src, group, s, slot, mode, upward):
+        (rows, landing), dev = (up_rows(mode), up) if upward else (down_rows(mode), dn)
+        return desc(kind, src.at[rows], r.at[group, s, slot, landing], s, slot, dev)
+
+    def copy(kind, s, slot, mode):
         if kind == K_YRE:
-            return desc(kind, d.at[s, 1, 0], r.at[Y_RE, s, slot], s, slot, outer)
-        if kind == K_ZIM_U:
-            return desc(kind, d.at[s, 1, 1, TOP], r.at[Z_IM, s, slot, BOT], s, slot, up)
-        if kind == K_ZIM_D:
-            return desc(kind, d.at[s, 1, 1, BOT], r.at[Z_IM, s, slot, TOP], s, slot, dn)
+            rows = first_rows(mode)
+            plane = 0 if s == 0 else 1 - core
+            return desc(kind, d.at[s, 1, plane, rows], r.at[Y_RE, s, slot, rows], s, slot, outer)
+        if kind in (K_ZIM_U, K_ZIM_D):
+            plane = 1 if s == 0 else 1 - core
+            return along_z(kind, d.at[s, 1, plane], Z_IM, s, slot, FIRST if mode == FIRST else USUAL, kind == K_ZIM_U)
         if kind == K_M:
-            return desc(kind, d.at[s, 0, 1 - core], r.at[M_RS, s, slot], s, slot, mate)
-        if kind == K_ZM_U:
-            return desc(kind, a.at[2, s, TOP], r.at[Z_M, s, slot, BOT], s, slot, up)
-        if kind == K_ZM_D:
-            return desc(kind, a.at[2, s, BOT], r.at[Z_M, s, slot, TOP], s, slot, dn)
-        if kind == K_ZRE_U:
-            return desc(kind, a.at[0, s, TOP], r.at[Z_RE, s, slot, BOT], s, slot, up)
-        if kind == K_ZRE_D:
-            return desc(kind, a.at[0, s, BOT], r.at[Z_RE, s, slot, TOP], s, slot, dn)
-        if kind == K_YIM:
-            return desc(kind, a.at[1, s], r.at[Y_IM, s, slot], s, slot, outer)
-        return desc(kind, objects[s].at[0, core], objects[s].at[0, core], s, slot, mate)
-
-    senders = {
-        K_YRE: has_o, K_ZIM_U: has_u, K_ZIM_D: has_d, K_M: None, K_ZM_U: has_u, K_ZM_D: has_d,
-        K_ZRE_U: has_u, K_ZRE_D: has_d, K_YIM: has_o, K_P3: None,
-    }
-    receivers = dict(senders)
-    for ku, kd in ((K_ZIM_U, K_ZIM_D), (K_ZM_U, K_ZM_D), (K_ZRE_U, K_ZRE_D)):
-        receivers[ku], receivers[kd] = has_d, has_u
+            rows = first_rows(mode)
+            return desc(kind, d.at[s, 0, 1 - core, rows], r.at[M_RS, s, slot, rows], s, slot, mate)
+        if kind in (K_ZM_U, K_ZM_D):
+            return along_z(kind, a.at[2, s], Z_M, s, slot, mode, kind == K_ZM_U)
+        if kind in (K_ZRE_U, K_ZRE_D):
+            return along_z(kind, a.at[0, s], Z_RE, s, slot, mode, kind == K_ZRE_U)
+        rows = last_rows(mode)
+        if kind == K_YIM and s == 0:
+            return desc(kind, a.at[1, s, rows], r.at[Y_IM, s, slot, rows], s, slot, outer)
+        half, dev = (1, outer) if kind == K_YIM else (0, mate)
+        return desc(kind, objects[s].at[half, core, rows], objects[s].at[half, core, rows], s, slot, dev)
+
+    def landed(kind, s, slot, mode):
+        if kind == K_P3 or (kind == K_YIM and s == 1):
+            rows = last_rows(mode)
+            half, dev = (1, outer) if kind == K_YIM else (0, mate)
+            return desc(kind, objects[s].at[half, core, rows], objects[s].at[half, 1 - core, rows], s, slot, dev)
+        return copy(kind, s, slot, mode)
+
+    def both_of(x, y):
+        return jnp.logical_and(x, y)
+
+    has_no = jnp.logical_not(has_o)
+    senders = [
+        {K_YRE: has_o, K_ZIM_U: has_u, K_ZIM_D: has_d, K_M: None, K_ZM_U: has_u, K_ZM_D: has_d,
+         K_ZRE_U: has_u, K_ZRE_D: has_d, K_YIM: has_o, K_P3: None},
+    ]
+    senders.append({**senders[0], K_ZIM_U: both_of(has_u, has_no), K_ZIM_D: both_of(has_d, has_no)})
+    other_way = {K_ZIM_U: K_ZIM_D, K_ZM_U: K_ZM_D, K_ZRE_U: K_ZRE_D}
+    other_way.update({v: k for k, v in other_way.items()})
 
     def guarded(cond, fn):
         if cond is None:
@@ -137,68 +166,111 @@
         else:
             pl.when(cond)(fn)
 
-    def send(kind, s, slot):
-        guarded(senders[kind], lambda: copy(kind, s, slot).start())
-
-    def recv(kind, s, slot):
-        if kind == K_P3:
-            desc(kind, objects[s].at[0, core], objects[s].at[0, 1 - core], s, slot, mate).wait_recv()
-        else:
-            guarded(receivers[kind], lambda: copy(kind, s, slot).wait_recv())
-
-    def sent(kind, s, slot):
-        guarded(senders[kind], lambda: copy(kind, s, slot).wait_send())
-
-    def start(s, slot):
-        send(K_M, s, slot)
-        send(K_YRE, s, slot)
-        send(K_ZIM_U, s, slot)
-        send(K_ZIM_D, s, slot)
-
-    def mid_m(s, slot):
-        recv(K_M, s, slot)
+    def send(kind, s, slot, mode):
+        guarded(senders[s][kind], lambda: copy(kind, s, slot, mode).start())
+
+    def recv(kind, s, slot, mode):
+        guarded(senders[s][other_way.get(kind, kind)], lambda: landed(kind, s, slot, mode).wait_recv())
+
+    def sent(kind, s, slot, mode):
+        guarded(senders[s][kind], lambda: copy(kind, s, slot, mode).wait_send())
+
+    def start(s, slot, mode):
+        send(K_M, s, slot, mode)
+        send(K_YRE, s, slot, mode)
+        send(K_ZIM_U, s, slot, mode)
+        send(K_ZIM_D, s, slot, mode)
+
+    def mid_m(s, slot, mode):
+        recv(K_M, s, slot, mode)
         a[2, s] = d[s, 0, core] + r[M_RS, s, slot]
-        send(K_ZM_U, s, slot)
-        send(K_ZM_D, s, slot)
-
-    def mid_re(s, slot):
-        recv(K_YRE, s, slot)
-        a[0, s] = d[s, 1, 0] + r[Y_RE, s, slot]
-        send(K_ZRE_U, s, slot)
-        send(K_ZRE_D, s, slot)
-
-    def mid_im(s, slot):
-        recv(K_ZIM_U, s, slot)
-        recv(K_ZIM_D, s, slot)
-        a[1, s] = d[s, 1, 1] + r[Z_IM, s, slot]
-        send(K_YIM, s, slot)
-
-    def mid_back(s, slot):
-        recv(K_ZM_U, s, slot)
-        recv(K_ZM_D, s, slot)
+        send(K_ZM_U, s, slot, mode)
+        send(K_ZM_D, s, slot, mode)
+
+    def mid_re(s, slot, mode):
+        recv(K_YRE, s, slot, mode)
+        a[0, s] = d[s, 1, 0 if s == 0 else core] + r[Y_RE, s, slot]
+        send(K_ZRE_U, s, slot, mode)
+        send(K_ZRE_D, s, slot, mode)
+
+    def mid_im(slot, mode):
+        recv(K_ZIM_U, 0, slot, mode)
+        recv(K_ZIM_D, 0, slot, mode)
+        a[1, 0] = d[0, 1, 1] + r[Z_IM, 0, slot]
+        send(K_YIM, 0, slot, mode)
+
+    def mid_back(s, slot, mode):
+        recv(K_ZM_U, s, slot, mode)
+        recv(K_ZM_D, s, slot, mode)
         objects[s][0, core] = objects[s][0, core] + (a[2, s] + r[Z_M, s, slot])
-        send(K_P3, s, slot)
-
-    def finish(s, slot):
-        recv(K_ZRE_U, s, slot)
-        recv(K_ZRE_D, s, slot)
-        objects[s][1, 0] = objects[s][1, 0] + (a[0, s] + r[Z_RE, s, slot])
-        recv(K_YIM, s, slot)
-        objects[s][1, 1] = objects[s][1, 1] + (a[1, s] + r[Y_IM, s, slot])
-        recv(K_P3, s, slot)
+        send(K_P3, s, slot, mode)
+
+    def outer_back(slot, mode):
+        recv(K_ZRE_U, 1, slot, mode)
+        recv(K_ZRE_D, 1, slot, mode)
+        o1[1, core] = o1[1, core] + (a[0, 1] + r[Z_RE, 1, slot])
+        send(K_YIM, 1, slot, mode)
+        recv(K_ZIM_U, 1, slot, mode)
+        recv(K_ZIM_D, 1, slot, mode)
+
+        @pl.when(has_no)
+        def _():
+            o1[1, 1 - core] = o1[1, 1 - core] + (d[1, 1, 1 - core] + r[Z_IM, 1, slot])
+
+    def finish_0(slot, mode):
+        recv(K_ZRE_U, 0, slot, mode)
+        recv(K_ZRE_D, 0, slot, mode)
+        o0[1, 0] = o0[1, 0] + (a[0, 0] + r[Z_RE, 0, slot])
+        recv(K_YIM, 0, slot, mode)
+        o0[1, 1] = o0[1, 1] + (a[1, 0] + r[Y_IM, 0, slot])
+        recv(K_P3, 0, slot, mode)
         for kind in range(10):
-            sent(kind, s, slot)
-
-    def exchange(slot):
-        mid_m(1, slot)
-        mid_m(0, slot)
-        mid_re(1, slot)
-        mid_im(1, slot)
-        mid_re(0, slot)
-        mid_im(0, slot)
-        mid_back(0, slot)
-        mid_back(1, slot)
-        finish(0, slot)
+            sent(kind, 0, slot, mode)
+
+    def drain_1(slot, mode):
+        for kind in range(8):
+            sent(kind, 1, slot, mode)
+
+    def finish_1(slot, mode):
+        for kind in (K_P3, K_YIM):
+            recv(kind, 1, slot, mode)
+            sent(kind, 1, slot, mode)
+
+    def exchange(slot, mode):
+        mid_m(1, slot, mode)
+        mid_m(0, slot, mode)
+        mid_re(1, slot, mode)
+        mid_re(0, slot, mode)
+        mid_im(slot, mode)
+        mid_back(1, slot, mode)
+        mid_back(0, slot, mode)
+        outer_back(slot, mode)
+        drain_1(slot, mode)
+        if mode == LAST:
+            finish_1(slot, mode)
+            give(1)
+        finish_0(slot, mode)
+
+    def send_home(s):
+        return pltpu.make_async_remote_copy(
+            src_ref=fin.at[s],
+            dst_ref=out.at[s],
+            send_sem=out_send.at[s],
+            recv_sem=out_recv.at[s],
+            device_id=home,
+            device_id_type=MESH,
+        )
+
+    def give(s):
+        for c in range(2):
+            left = objects[s][hl, c, pl.ds(H, N), :]
+            right = objects[s][hr, c, pl.ds(H, N), :]
+            fin[s, c] = pltpu.roll(jnp.where(lane >= H, left, right), H, 1)
+        pl.when(moved)(lambda: send_home(s).start())
+
+        @pl.when(stays)
+        def _():
+            out[s] = fin[s]
 
     inputs = [(offs_in, offs), (cnt_in, cnt)]
     inputs += [(obj.at[s], tile.at[s]) for s in range(2)]
@@ -232,38 +304,59 @@
         return 4 + b, inten_in.at[pl.ds(BATCH * b, BATCH)], inten.at[pl.ds(BATCH * b, BATCH)]
 
     consts = [(probe_in, probe), (prop_in, prop), (w_in, w)]
+    barrier = pltpu.get_barrier_semaphore()
+    greet = ((None, mate), (has_u, up), (has_d, dn), (has_o, outer), (moved, home), (moved, worker))
+    for cond, dev in greet:
+        guarded(cond, lambda dev=dev: pl.semaphore_signal(barrier, inc=1, device_id=dev, device_id_type=MESH))
     for i, (src, dst) in enumerate(consts):
         pltpu.make_async_copy(src, dst, lsem.at[i]).start()
-
-    barrier = pltpu.get_barrier_semaphore()
-    greet = ((None, mate), (has_u, up), (has_d, dn), (has_o, outer), (moved, home), (moved, worker))
-    r[...] = jnp.zeros_like(r)
+    count = 1 + sum(jnp.where(cond, 1, 0) for cond, _ in greet[1:])
+    pl.semaphore_wait(barrier, count)
+    for i in (2, 0, 1):
+        pass_start(i, *inputs[i])
     for o in objects:
         o[...] = jnp.zeros_like(o)
     d[...] = jnp.zeros_like(d)
     z[...] = jnp.zeros_like(z)
-    for cond, dev in greet:
-        guarded(cond, lambda dev=dev: pl.semaphore_signal(barrier, inc=1, device_id=dev, device_id_type=MESH))
-    count = 1 + sum(jnp.where(cond, 1, 0) for cond, _ in greet[1:])
-    pl.semaphore_wait(barrier, count)
-    for i in range(4):
-        pass_start(i, *inputs[i])
-    pass_start(*frames(0))
+    for group, rows in ((Y_RE, ((0, H), (3 * H, H))), (M_RS, ((0, H), (3 * H, H)))):
+        for first, n in rows:
+            r[group, :, 0, pl.ds(first, n)] = jnp.zeros((2, n, N), F32)
+    for group in (Z_IM, Z_M, Z_RE):
+        r[group, :, 0, pl.ds(H, N)] = jnp.zeros((2, N, N), F32)
+
+    @pl.when(gx == 0)
+    def _():
+        for group in (Z_IM, Z_M, Z_RE):
+            r[group, :, :, TOP] = jnp.zeros((2, 2, N, N), F32)
+
+    @pl.when(gx == 7)
+    def _():
+        for group in (Z_IM, Z_M, Z_RE):
+            r[group, :, :, BOT] = jnp.zeros((2, 2, N, N), F32)
+
+    @pl.when(has_no)
+    def _():
+        for group in (Y_RE, Y_IM):
+            r[group] = jnp.zeros((2, 2, 2 * N, N), F32)
+
+    for i, (src, dst) in enumerate(consts):
+        pltpu.make_async_copy(src, dst, lsem.at[i]).wait()
+    q[0] = jnp.cos(prop[...])
+    q[1] = jnp.sin(prop[...])
+    pass_start(3, *inputs[3])
 
     for s in (0, 1):
         pass_wait(2 + s, *inputs[2 + s])
+        if s == 1:
+            pass_start(*frames(0))
         for c in range(2):
             cells = pltpu.roll(tile[s, c], H, 1)
             d[s, hl, c, pl.ds(H, N)] = jnp.where(lane >= H, cells, 0.0)
             d[s, hr, c, pl.ds(H, N)] = jnp.where(lane < H, cells, 0.0)
-        start(s, 0)
-    for i, (src, dst) in enumerate(consts):
-        pltpu.make_async_copy(src, dst, lsem.at[i]).wait()
+        start(s, 0, FIRST)
     for i in range(2):
         pass_wait(i, *inputs[i])
-    q[0] = jnp.cos(prop[...])
-    q[1] = jnp.sin(prop[...])
-    exchange(0)
+    exchange(0, FIRST)
 
     def split(x):
         hi = x.astype(BF16)
@@ -323,7 +416,7 @@
         for m in range(BATCH):
             psi[m, 0] = re[m]
             psi[m, 1] = im[m]
-        finish(1, before)
+        finish_1(before, USUAL)
         both = []
         for m in range(BATCH):
             r0, q0, _ = places[m]
@@ -336,42 +429,20 @@
         re, im = transform([excess[m] * re[m] for m in range(BATCH)], [excess[m] * im[m] for m in range(BATCH)], 1)
         both = [cmul(psi[m, 0], -psi[m, 1], re[m], im[m]) for m in range(BATCH)]
         scatter(1, places, ([x for x, _ in both], [y for _, y in both]))
-        start(1, slot)
+        start(1, slot, USUAL)
         both = [cmul(pat[m, 0], -pat[m, 1], re[m], im[m]) for m in range(BATCH)]
         re, im = transform([x for x, _ in both], [y for _, y in both], 0)
         both = [cmul(re[m], im[m], q[0], -q[1]) for m in range(BATCH)]
         re, im = transform([x for x, _ in both], [y for _, y in both], 1)
         both = [cmul(re[m], im[m], pr, -pi) for m in range(BATCH)]
         scatter(0, places, ([x for x, _ in both], [y for _, y in both]))
-        start(0, slot)
-        exchange(slot)
+        start(0, slot, USUAL)
+        pl.when(b < NB - 1)(lambda: exchange(slot, USUAL))
+        pl.when(b == NB - 1)(lambda: exchange(slot, LAST))
         return carry
-
-    def send_home(s):
-        return pltpu.make_async_remote_copy(
-            src_ref=fin.at[s],
-            dst_ref=out.at[s],
-            send_sem=out_send.at[s],
-            recv_sem=out_recv.at[s],
-            device_id=home,
-            device_id_type=MESH,
-        )
-
-    def give(s):
-        for c in range(2):
-            left = objects[s][hl, c, pl.ds(H, N), :]
-            right = objects[s][hr, c, pl.ds(H, N), :]
-            fin[s, c] = pltpu.roll(jnp.where(lane >= H, left, right), H, 1)
-        pl.when(moved)(lambda: send_home(s).start())
-
-        @pl.when(stays)
-        def _():
-            out[s] = fin[s]
 
     lax.fori_loop(0, NB, batch, 0)
     give(0)
-    finish(1, NB % 2)
-    give(1)
     for s in range(2):
         @pl.when(moved)
         def _():
@@ -416,7 +487,7 @@
                 pltpu.SemaphoreType.DMA((3,)),
             ],
             compiler_params=pltpu.CompilerParams(
-                collective_id=0, has_side_effects=True, vmem_limit_bytes=48 * 1024 * 1024
+                collective_id=0, has_side_effects=True, vmem_limit_bytes=58 * 1024 * 1024
             ),
         )(
             offsets[0, 0].T, counts, object_field, probe, propagator, intensity[0, 0], jnp.asarray(tables),

time: 127 us -> 129 us (1.016)
  the two profiles are of different devices: /device:TPU:6 before, /device:TPU:55 now
where the time goes in v3:
time: 129 us
  Pallas kernels  127 us (98%)
  local copies, waits for them, and re-layouts  1.67 us (1%)
    pallas_call x1, Pallas kernels, local(): pl.pallas_call(kernel, out_shape=jax.ShapeDtypeStruct((2, 2, N, N), F32),...  127 us

profile of v3, /device:TPU:55, one launch (start us, length us, event | category | flops | bytes accessed | tf_op | source)
XLA Modules:
  0.0 128.8 jit_solution(11175366062726986171)
XLA Ops:
  0.7 126.5 %shard_map.73 = f32[2,2,128,128]{3,2,1,0:T(8,128)} custom-call(s32[2,12]{1,0:T(2,128)} %bitcast.5, s32[1,1]{1,0:T(1,128)S(6)} %copy.9.cnt_in, f32[2,2,128,128]{3,2,1,0:T(8,128)} %obj.1, f32[2,128,128]{2,1,0:T(8,128)} %probe_in.1, f32[128,128]{1,0:T(8,128)} %prop_in.1, f32[12,128,128]{2,1,0:T(8,128)} %bitcast.4, bf16[2,2,256,256]{3,2,1,0:T(8,128)(2,1)} %constant.2.clone.w_in), custom_call_target="tpu_custom_call" | custom-call | tf_op jit(solution)/shard_map/pallas_call | solution.py:458
  127.2 1.7 %copy.10 = f32[2,2,128,128]{3,2,1,0:T(8,128)} copy(f32[2,2,128,128]{3,2,1,0:T(8,128)} %shard_map.73) | data formatting | bytes 524288

commit v4 on v3

--- a/solution.py
+++ b/solution.py
@@ -49,14 +49,14 @@
 def tile_of(gx, gy):
     hi_x, z, lo_x, y, core = parts(gx, gy)
     lo_x = lax.rem(lo_x + hi_x, 2)
-    z = jnp.where(hi_x == 1, 3 - z, z)
+    z = jnp.where(hi_x == 0, 3 - z, z)
     y = jnp.where(lo_x == 1, 3 - y, y)
     return place(hi_x, lo_x, y, z, core)
 
 
 def device_of(gx, gy):
     hi_x, z, lo_x, y, core = parts(gx, gy)
-    z = jnp.where(hi_x == 1, 3 - z, z)
+    z = jnp.where(hi_x == 0, 3 - z, z)
     y = jnp.where(lo_x == 1, 3 - y, y)
     return place(hi_x, lax.rem(lo_x + hi_x, 2), y, z, core)
 
@@ -123,40 +123,33 @@
     def copy(kind, s, slot, mode):
         if kind == K_YRE:
             rows = first_rows(mode)
-            plane = 0 if s == 0 else 1 - core
-            return desc(kind, d.at[s, 1, plane, rows], r.at[Y_RE, s, slot, rows], s, slot, outer)
+            return desc(kind, d.at[s, 1, 0, rows], r.at[Y_RE, s, slot, rows], s, slot, outer)
         if kind in (K_ZIM_U, K_ZIM_D):
-            plane = 1 if s == 0 else 1 - core
-            return along_z(kind, d.at[s, 1, plane], Z_IM, s, slot, FIRST if mode == FIRST else USUAL, kind == K_ZIM_U)
+            return along_z(kind, d.at[s, 1, 1], Z_IM, s, slot, FIRST if mode == FIRST else USUAL, kind == K_ZIM_U)
         if kind == K_M:
             rows = first_rows(mode)
             return desc(kind, d.at[s, 0, 1 - core, rows], r.at[M_RS, s, slot, rows], s, slot, mate)
         if kind in (K_ZM_U, K_ZM_D):
-            return along_z(kind, a.at[2, s], Z_M, s, slot, mode, kind == K_ZM_U)
+            early = s == 1 and mode == LAST
+            return along_z(kind, a.at[2, s], Z_M, s, slot, USUAL if early else mode, kind == K_ZM_U)
         if kind in (K_ZRE_U, K_ZRE_D):
             return along_z(kind, a.at[0, s], Z_RE, s, slot, mode, kind == K_ZRE_U)
         rows = last_rows(mode)
-        if kind == K_YIM and s == 0:
+        if kind == K_YIM:
             return desc(kind, a.at[1, s, rows], r.at[Y_IM, s, slot, rows], s, slot, outer)
-        half, dev = (1, outer) if kind == K_YIM else (0, mate)
-        return desc(kind, objects[s].at[half, core, rows], objects[s].at[half, core, rows], s, slot, dev)
+        return desc(kind, objects[s].at[0, core, rows], objects[s].at[0, core, rows], s, slot, mate)
 
     def landed(kind, s, slot, mode):
-        if kind == K_P3 or (kind == K_YIM and s == 1):
+        if kind == K_P3:
             rows = last_rows(mode)
-            half, dev = (1, outer) if kind == K_YIM else (0, mate)
-            return desc(kind, objects[s].at[half, core, rows], objects[s].at[half, 1 - core, rows], s, slot, dev)
+            return desc(kind, objects[s].at[0, core, rows], objects[s].at[0, 1 - core, rows], s, slot, mate)
         return copy(kind, s, slot, mode)
 
-    def both_of(x, y):
-        return jnp.logical_and(x, y)
-
     has_no = jnp.logical_not(has_o)
-    senders = [
-        {K_YRE: has_o, K_ZIM_U: has_u, K_ZIM_D: has_d, K_M: None, K_ZM_U: has_u, K_ZM_D: has_d,
-         K_ZRE_U: has_u, K_ZRE_D: has_d, K_YIM: has_o, K_P3: None},
-    ]
-    senders.append({**senders[0], K_ZIM_U: both_of(has_u, has_no), K_ZIM_D: both_of(has_d, has_no)})
+    senders = {
+        K_YRE: has_o, K_ZIM_U: has_u, K_ZIM_D: has_d, K_M: None, K_ZM_U: has_u, K_ZM_D: has_d,
+        K_ZRE_U: has_u, K_ZRE_D: has_d, K_YIM: has_o, K_P3: None,
+    }
     other_way = {K_ZIM_U: K_ZIM_D, K_ZM_U: K_ZM_D, K_ZRE_U: K_ZRE_D}
     other_way.update({v: k for k, v in other_way.items()})
 
@@ -167,13 +160,13 @@
             pl.when(cond)(fn)
 
     def send(kind, s, slot, mode):
-        guarded(senders[s][kind], lambda: copy(kind, s, slot, mode).start())
+        guarded(senders[kind], lambda: copy(kind, s, slot, mode).start())
 
     def recv(kind, s, slot, mode):
-        guarded(senders[s][other_way.get(kind, kind)], lambda: landed(kind, s, slot, mode).wait_recv())
+        guarded(senders[other_way.get(kind, kind)], lambda: landed(kind, s, slot, mode).wait_recv())
 
     def sent(kind, s, slot, mode):
-        guarded(senders[s][kind], lambda: copy(kind, s, slot, mode).wait_send())
+        guarded(senders[kind], lambda: copy(kind, s, slot, mode).wait_send())
 
     def start(s, slot, mode):
         send(K_M, s, slot, mode)
@@ -189,15 +182,15 @@
 
     def mid_re(s, slot, mode):
         recv(K_YRE, s, slot, mode)
-        a[0, s] = d[s, 1, 0 if s == 0 else core] + r[Y_RE, s, slot]
+        a[0, s] = d[s, 1, 0] + r[Y_RE, s, slot]
         send(K_ZRE_U, s, slot, mode)
         send(K_ZRE_D, s, slot, mode)
 
-    def mid_im(slot, mode):
-        recv(K_ZIM_U, 0, slot, mode)
-        recv(K_ZIM_D, 0, slot, mode)
-        a[1, 0] = d[0, 1, 1] + r[Z_IM, 0, slot]
-        send(K_YIM, 0, slot, mode)
+    def mid_im(s, slot, mode):
+        recv(K_ZIM_U, s, slot, mode)
+        recv(K_ZIM_D, s, slot, mode)
+        a[1, s] = d[s, 1, 1] + r[Z_IM, s, slot]
+        send(K_YIM, s, slot, mode)
 
     def mid_back(s, slot, mode):
         recv(K_ZM_U, s, slot, mode)
@@ -205,51 +198,28 @@
         objects[s][0, core] = objects[s][0, core] + (a[2, s] + r[Z_M, s, slot])
         send(K_P3, s, slot, mode)
 
-    def outer_back(slot, mode):
-        recv(K_ZRE_U, 1, slot, mode)
-        recv(K_ZRE_D, 1, slot, mode)
-        o1[1, core] = o1[1, core] + (a[0, 1] + r[Z_RE, 1, slot])
-        send(K_YIM, 1, slot, mode)
-        recv(K_ZIM_U, 1, slot, mode)
-        recv(K_ZIM_D, 1, slot, mode)
-
-        @pl.when(has_no)
-        def _():
-            o1[1, 1 - core] = o1[1, 1 - core] + (d[1, 1, 1 - core] + r[Z_IM, 1, slot])
-
-    def finish_0(slot, mode):
-        recv(K_ZRE_U, 0, slot, mode)
-        recv(K_ZRE_D, 0, slot, mode)
-        o0[1, 0] = o0[1, 0] + (a[0, 0] + r[Z_RE, 0, slot])
-        recv(K_YIM, 0, slot, mode)
-        o0[1, 1] = o0[1, 1] + (a[1, 0] + r[Y_IM, 0, slot])
-        recv(K_P3, 0, slot, mode)
+    def finish(s, slot, mode):
+        recv(K_ZRE_U, s, slot, mode)
+        recv(K_ZRE_D, s, slot, mode)
+        objects[s][1, 0] = objects[s][1, 0] + (a[0, s] + r[Z_RE, s, slot])
+        recv(K_YIM, s, slot, mode)
+        objects[s][1, 1] = objects[s][1, 1] + (a[1, s] + r[Y_IM, s, slot])
+        recv(K_P3, s, slot, mode)
         for kind in range(10):
-            sent(kind, 0, slot, mode)
-
-    def drain_1(slot, mode):
-        for kind in range(8):
-            sent(kind, 1, slot, mode)
-
-    def finish_1(slot, mode):
-        for kind in (K_P3, K_YIM):
-            recv(kind, 1, slot, mode)
-            sent(kind, 1, slot, mode)
+            sent(kind, s, slot, mode)
 
     def exchange(slot, mode):
-        mid_m(1, slot, mode)
         mid_m(0, slot, mode)
         mid_re(1, slot, mode)
+        mid_im(1, slot, mode)
         mid_re(0, slot, mode)
-        mid_im(slot, mode)
+        mid_im(0, slot, mode)
         mid_back(1, slot, mode)
         mid_back(0, slot, mode)
-        outer_back(slot, mode)
-        drain_1(slot, mode)
         if mode == LAST:
-            finish_1(slot, mode)
+            finish(1, slot, mode)
             give(1)
-        finish_0(slot, mode)
+        finish(0, slot, mode)
 
     def send_home(s):
         return pltpu.make_async_remote_copy(
@@ -345,18 +315,28 @@
     q[1] = jnp.sin(prop[...])
     pass_start(3, *inputs[3])
 
-    for s in (0, 1):
+    def begin(s):
         pass_wait(2 + s, *inputs[2 + s])
-        if s == 1:
-            pass_start(*frames(0))
         for c in range(2):
             cells = pltpu.roll(tile[s, c], H, 1)
             d[s, hl, c, pl.ds(H, N)] = jnp.where(lane >= H, cells, 0.0)
             d[s, hr, c, pl.ds(H, N)] = jnp.where(lane < H, cells, 0.0)
         start(s, 0, FIRST)
+
+    begin(0)
+    mid_m(0, 0, FIRST)
+    begin(1)
+    pass_start(*frames(0))
+    mid_re(0, 0, FIRST)
+    mid_im(0, 0, FIRST)
+    mid_m(1, 0, FIRST)
+    mid_back(0, 0, FIRST)
+    mid_re(1, 0, FIRST)
+    mid_im(1, 0, FIRST)
+    mid_back(1, 0, FIRST)
     for i in range(2):
         pass_wait(i, *inputs[i])
-    exchange(0, FIRST)
+    finish(0, 0, FIRST)
 
     def split(x):
         hi = x.astype(BF16)
@@ -416,7 +396,8 @@
         for m in range(BATCH):
             psi[m, 0] = re[m]
             psi[m, 1] = im[m]
-        finish_1(before, USUAL)
+        pl.when(b == 0)(lambda: finish(1, before, FIRST))
+        pl.when(b > 0)(lambda: finish(1, before, USUAL))
         both = []
         for m in range(BATCH):
             r0, q0, _ = places[m]
@@ -437,6 +418,7 @@
         both = [cmul(re[m], im[m], pr, -pi) for m in range(BATCH)]
         scatter(0, places, ([x for x, _ in both], [y for _, y in both]))
         start(0, slot, USUAL)
+        mid_m(1, slot, USUAL)
         pl.when(b < NB - 1)(lambda: exchange(slot, USUAL))
         pl.when(b == NB - 1)(lambda: exchange(slot, LAST))
         return carry

time: 129 us -> 117 us (0.907)
  the two profiles are of different devices: /device:TPU:55 before, /device:TPU:6 now
where the time goes in v4:
time: 117 us; the launch traced here: 116 us
  Pallas kernels  113 us (97%)
  local copies, waits for them, and re-layouts  1.67 us (1%)
    pallas_call x1, Pallas kernels, local(): pl.pallas_call(kernel, out_shape=jax.ShapeDtypeStruct((2, 2, N, N), F32),...  113 us

profile of v4, /device:TPU:6, one launch (start us, length us, event | category | flops | bytes accessed | tf_op | source)
XLA Modules:
  0.0 115.8 jit_solution(12833511796013307527)
XLA Ops:
  0.7 113.5 %shard_map.73 = f32[2,2,128,128]{3,2,1,0:T(8,128)} custom-call(s32[2,12]{1,0:T(2,128)} %bitcast.5, s32[1,1]{1,0:T(1,128)S(6)} %copy.9.cnt_in, f32[2,2,128,128]{3,2,1,0:T(8,128)} %obj.1, f32[2,128,128]{2,1,0:T(8,128)} %probe_in.1, f32[128,128]{1,0:T(8,128)} %prop_in.1, f32[12,128,128]{2,1,0:T(8,128)} %bitcast.4, bf16[2,2,256,256]{3,2,1,0:T(8,128)(2,1)} %constant.2.clone.w_in), custom_call_target="tpu_custom_call" | custom-call | tf_op jit(solution)/shard_map/pallas_call | solution.py:440
  114.2 1.7 %copy.10 = f32[2,2,128,128]{3,2,1,0:T(8,128)} copy(f32[2,2,128,128]{3,2,1,0:T(8,128)} %shard_map.73) | data formatting | bytes 524288

commit v5 on v4

--- a/solution.py
+++ b/solution.py
@@ -67,7 +67,7 @@
 
 def kernel(
     offs_in, cnt_in, obj, probe_in, prop_in, inten_in, w_in, out,
-    o0, o1, d, z, r, a, q, psi, pat, tile, inten, fin, probe, prop, w, offs, cnt,
+    o0, o1, d, z, r, a, q, psi, pat, tile, inten, fin, goal, probe, prop, w, offs, cnt,
     ssem, rsem, in_send, in_recv, out_send, out_recv, lsem,
 ):
     objects = (o0, o1)
@@ -210,12 +210,13 @@
 
     def exchange(slot, mode):
         mid_m(0, slot, mode)
-        mid_re(1, slot, mode)
+        mid_m(1, slot, USUAL)
         mid_im(1, slot, mode)
         mid_re(0, slot, mode)
         mid_im(0, slot, mode)
+        mid_re(1, slot, mode)
+        mid_back(0, slot, mode)
         mid_back(1, slot, mode)
-        mid_back(0, slot, mode)
         if mode == LAST:
             finish(1, slot, mode)
             give(1)
@@ -311,8 +312,8 @@
 
     for i, (src, dst) in enumerate(consts):
         pltpu.make_async_copy(src, dst, lsem.at[i]).wait()
-    q[0] = jnp.cos(prop[...])
-    q[1] = jnp.sin(prop[...])
+    q[0] = jnp.cos(prop[...]).T
+    q[1] = jnp.sin(prop[...]).T
     pass_start(3, *inputs[3])
 
     def begin(s):
@@ -343,17 +344,16 @@
         return hi, (x - hi.astype(F32)).astype(BF16)
 
     def transform(re, im, inverse):
-        x = jnp.concatenate([jnp.concatenate([re[m], im[m]], 1) for m in range(BATCH)], 0)
-        hi, lo = split(x)
         right = jnp.concatenate([w[inverse, 0], w[inverse, 0], w[inverse, 1]], 0)
-        y = jnp.dot(jnp.concatenate([hi, lo, hi], 1), right, preferred_element_type=F32)
-        x = jnp.concatenate(
-            [jnp.concatenate([y[:N, :N], y[N:, :N]], 1), jnp.concatenate([y[:N, N:], y[N:, N:]], 1)], 0
-        )
-        hi, lo = split(x)
-        left = jnp.concatenate([w[1 - inverse, 0], w[1 - inverse, 0], w[1 - inverse, 1]], 1)
-        y = jnp.dot(left, jnp.concatenate([hi, lo, hi], 0), preferred_element_type=F32)
-        return (y[:N, :N], y[:N, N:]), (y[N:, :N], y[N:, N:])
+
+        def product(x, y):
+            hi, lo = split(jnp.concatenate([x, y], 1))
+            z = jnp.dot(jnp.concatenate([hi, lo, hi], 1), right, preferred_element_type=F32)
+            return z[:, :N], z[:, N:]
+
+        first = [product(re[m], im[m]) for m in range(BATCH)]
+        second = [product(x.T, y.T) for x, y in first]
+        return [x for x, _ in second], [y for _, y in second]
 
     def patch(s, c, r0, q0):
         left = objects[s][hl, c, pl.ds(r0, N), :]
@@ -396,6 +396,9 @@
         for m in range(BATCH):
             psi[m, 0] = re[m]
             psi[m, 1] = im[m]
+        pass_wait(*frames(b))
+        for m in range(BATCH):
+            goal[m] = inten[b * BATCH + m].T
         pl.when(b == 0)(lambda: finish(1, before, FIRST))
         pl.when(b > 0)(lambda: finish(1, before, USUAL))
         both = []
@@ -405,8 +408,7 @@
                 pat[m, c] = patch(1, c, r0, q0)
             both.append(cmul(psi[m, 0], psi[m, 1], pat[m, 0], pat[m, 1]))
         re, im = transform([x for x, _ in both], [y for _, y in both], 0)
-        pass_wait(*frames(b))
-        excess = [re[m] * re[m] + im[m] * im[m] - inten[b * BATCH + m] for m in range(BATCH)]
+        excess = [re[m] * re[m] + im[m] * im[m] - goal[m] for m in range(BATCH)]
         re, im = transform([excess[m] * re[m] for m in range(BATCH)], [excess[m] * im[m] for m in range(BATCH)], 1)
         both = [cmul(psi[m, 0], -psi[m, 1], re[m], im[m]) for m in range(BATCH)]
         scatter(1, places, ([x for x, _ in both], [y for _, y in both]))
@@ -418,7 +420,6 @@
         both = [cmul(re[m], im[m], pr, -pi) for m in range(BATCH)]
         scatter(0, places, ([x for x, _ in both], [y for _, y in both]))
         start(0, slot, USUAL)
-        mid_m(1, slot, USUAL)
         pl.when(b < NB - 1)(lambda: exchange(slot, USUAL))
         pl.when(b == NB - 1)(lambda: exchange(slot, LAST))
         return carry
@@ -455,6 +456,7 @@
                 pltpu.VMEM((2, 2, N, N), F32),
                 pltpu.VMEM((NB * BATCH, N, N), F32),
                 pltpu.VMEM((2, 2, N, N), F32),
+                pltpu.VMEM((BATCH, N, N), F32),
                 pltpu.VMEM((2, N, N), F32),
                 pltpu.VMEM((N, N), F32),
                 pltpu.VMEM((2, 2, 2 * N, 2 * N), BF16),

time: 117 us -> 113 us (0.966)
  Pallas kernels: 113 us -> 109 us
    pallas_call x1, Pallas kernels: 113 us -> 109 us  [local(): pl.pallas_call(kernel, out_shape=jax.ShapeDtypeStruct((2, 2, N, N), F32),...]
where the time goes in v5:
time: 113 us; the launch traced here: 111 us
  Pallas kernels  109 us (96%)
  local copies, waits for them, and re-layouts  1.67 us (1%)
    pallas_call x1, Pallas kernels, local(): pl.pallas_call(kernel, out_shape=jax.ShapeDtypeStruct((2, 2, N, N), F32),...  109 us

profile of v5, /device:TPU:6, one launch (start us, length us, event | category | flops | bytes accessed | tf_op | source)
XLA Modules:
  0.0 111.3 jit_solution(6971119783447864829)
XLA Ops:
  0.7 109.0 %shard_map.73 = f32[2,2,128,128]{3,2,1,0:T(8,128)} custom-call(s32[2,12]{1,0:T(2,128)} %bitcast.5, s32[1,1]{1,0:T(1,128)S(6)} %copy.9.cnt_in, f32[2,2,128,128]{3,2,1,0:T(8,128)} %obj.1, f32[2,128,128]{2,1,0:T(8,128)} %probe_in.1, f32[128,128]{1,0:T(8,128)} %prop_in.1, f32[12,128,128]{2,1,0:T(8,128)} %bitcast.4, bf16[2,2,256,256]{3,2,1,0:T(8,128)(2,1)} %constant.2.clone.w_in), custom_call_target="tpu_custom_call" | custom-call | tf_op jit(solution)/shard_map/pallas_call | solution.py:441
  109.6 1.7 %copy.10 = f32[2,2,128,128]{3,2,1,0:T(8,128)} copy(f32[2,2,128,128]{3,2,1,0:T(8,128)} %shard_map.73) | data formatting | bytes 524288

commit v6 on v5

--- a/solution.py
+++ b/solution.py
@@ -20,6 +20,8 @@
 
 Y_RE, Z_IM, M_RS, Z_M, Z_RE, Y_IM = range(6)
 K_YRE, K_ZIM_U, K_ZIM_D, K_M, K_ZM_U, K_ZM_D, K_ZRE_U, K_ZRE_D, K_YIM, K_P3 = range(10)
+K_YRE_T, K_YRE_B, K_ZIM_U2, K_ZIM_D2, K_ZRE_U2, K_ZRE_D2, K_YIM_T, K_YIM_B = range(10, 18)
+KINDS = 18
 FIRST, USUAL, LAST = range(3)
 ALL = pl.ds(0, 2 * N)
 TOP = pl.ds(0, N)
@@ -116,16 +118,31 @@
     def last_rows(mode):
         return pl.ds(H, N) if mode == LAST else ALL
 
+    def live(kind, s, mode):
+        if s == 1:
+            return kind < 10
+        if kind in (K_YRE_T, K_YRE_B, K_ZIM_U2, K_ZIM_D2, K_ZRE_U2, K_ZRE_D2):
+            return mode != FIRST
+        if kind in (K_ZRE_U, K_ZRE_D, K_YIM_T, K_YIM_B):
+            return mode != LAST
+        return True
+
     def along_z(kind, src, group, s, slot, mode, upward):
         (rows, landing), dev = (up_rows(mode), up) if upward else (down_rows(mode), dn)
         return desc(kind, src.at[rows], r.at[group, s, slot, landing], s, slot, dev)
 
     def copy(kind, s, slot, mode):
-        if kind == K_YRE:
-            rows = first_rows(mode)
+        if kind in (K_YRE, K_YRE_T, K_YRE_B):
+            rows = first_rows(FIRST if s == 0 else mode)
+            rows = {K_YRE_T: pl.ds(0, H), K_YRE_B: pl.ds(3 * H, H)}.get(kind, rows)
             return desc(kind, d.at[s, 1, 0, rows], r.at[Y_RE, s, slot, rows], s, slot, outer)
+        if kind in (K_ZIM_U2, K_ZIM_D2):
+            return along_z(kind, d.at[s, 1, 1], Z_IM, s, slot, LAST, kind == K_ZIM_U2)
+        if kind in (K_ZRE_U2, K_ZRE_D2):
+            return along_z(kind, a.at[0, s], Z_RE, s, slot, LAST, kind == K_ZRE_U2)
         if kind in (K_ZIM_U, K_ZIM_D):
-            return along_z(kind, d.at[s, 1, 1], Z_IM, s, slot, FIRST if mode == FIRST else USUAL, kind == K_ZIM_U)
+            piece = FIRST if s == 0 or mode == FIRST else USUAL
+            return along_z(kind, d.at[s, 1, 1], Z_IM, s, slot, piece, kind == K_ZIM_U)
         if kind == K_M:
             rows = first_rows(mode)
             return desc(kind, d.at[s, 0, 1 - core, rows], r.at[M_RS, s, slot, rows], s, slot, mate)
@@ -133,9 +150,11 @@
             early = s == 1 and mode == LAST
             return along_z(kind, a.at[2, s], Z_M, s, slot, USUAL if early else mode, kind == K_ZM_U)
         if kind in (K_ZRE_U, K_ZRE_D):
-            return along_z(kind, a.at[0, s], Z_RE, s, slot, mode, kind == K_ZRE_U)
+            return along_z(kind, a.at[0, s], Z_RE, s, slot, FIRST if s == 0 else mode, kind == K_ZRE_U)
         rows = last_rows(mode)
-        if kind == K_YIM:
+        if kind in (K_YIM, K_YIM_T, K_YIM_B):
+            rows = pl.ds(H, N) if s == 0 else rows
+            rows = {K_YIM_T: pl.ds(0, H), K_YIM_B: pl.ds(3 * H, H)}.get(kind, rows)
             return desc(kind, a.at[1, s, rows], r.at[Y_IM, s, slot, rows], s, slot, outer)
         return desc(kind, objects[s].at[0, core, rows], objects[s].at[0, core, rows], s, slot, mate)
 
@@ -149,8 +168,10 @@
     senders = {
         K_YRE: has_o, K_ZIM_U: has_u, K_ZIM_D: has_d, K_M: None, K_ZM_U: has_u, K_ZM_D: has_d,
         K_ZRE_U: has_u, K_ZRE_D: has_d, K_YIM: has_o, K_P3: None,
+        K_YRE_T: has_o, K_YRE_B: has_o, K_ZIM_U2: has_u, K_ZIM_D2: has_d,
+        K_ZRE_U2: has_u, K_ZRE_D2: has_d, K_YIM_T: has_o, K_YIM_B: has_o,
     }
-    other_way = {K_ZIM_U: K_ZIM_D, K_ZM_U: K_ZM_D, K_ZRE_U: K_ZRE_D}
+    other_way = {K_ZIM_U: K_ZIM_D, K_ZM_U: K_ZM_D, K_ZRE_U: K_ZRE_D, K_ZIM_U2: K_ZIM_D2, K_ZRE_U2: K_ZRE_D2}
     other_way.update({v: k for k, v in other_way.items()})
 
     def guarded(cond, fn):
@@ -160,13 +181,16 @@
             pl.when(cond)(fn)
 
     def send(kind, s, slot, mode):
-        guarded(senders[kind], lambda: copy(kind, s, slot, mode).start())
+        if live(kind, s, mode):
+            guarded(senders[kind], lambda: copy(kind, s, slot, mode).start())
 
     def recv(kind, s, slot, mode):
-        guarded(senders[other_way.get(kind, kind)], lambda: landed(kind, s, slot, mode).wait_recv())
+        if live(kind, s, mode):
+            guarded(senders[other_way.get(kind, kind)], lambda: landed(kind, s, slot, mode).wait_recv())
 
     def sent(kind, s, slot, mode):
-        guarded(senders[kind], lambda: copy(kind, s, slot, mode).wait_send())
+        if live(kind, s, mode):
+            guarded(senders[kind], lambda: copy(kind, s, slot, mode).wait_send())
 
     def start(s, slot, mode):
         send(K_M, s, slot, mode)
@@ -192,6 +216,42 @@
         a[1, s] = d[s, 1, 1] + r[Z_IM, s, slot]
         send(K_YIM, s, slot, mode)
 
+    def rims_and_middle(mode):
+        rims, middle = [pl.ds(0, H), pl.ds(3 * H, H)], [pl.ds(H, N)]
+        return (rims, middle) if mode != FIRST else ([], [ALL])
+
+    def re_first(slot, mode):
+        recv(K_YRE, 0, slot, mode)
+        for rows in rims_and_middle(mode)[1]:
+            a[0, 0, rows] = d[0, 1, 0, rows] + r[Y_RE, 0, slot, rows]
+        send(K_ZRE_U, 0, slot, mode)
+        send(K_ZRE_D, 0, slot, mode)
+
+    def re_second(slot, mode):
+        recv(K_YRE_T, 0, slot, mode)
+        recv(K_YRE_B, 0, slot, mode)
+        for rows in rims_and_middle(mode)[0]:
+            a[0, 0, rows] = d[0, 1, 0, rows] + r[Y_RE, 0, slot, rows]
+        send(K_ZRE_U2, 0, slot, mode)
+        send(K_ZRE_D2, 0, slot, mode)
+
+    def im_first(slot, mode):
+        recv(K_ZIM_U2, 0, slot, mode)
+        recv(K_ZIM_D2, 0, slot, mode)
+        if mode != FIRST:
+            a[1, 0, pl.ds(H, N)] = d[0, 1, 1, pl.ds(H, N)] + r[Z_IM, 0, slot, pl.ds(H, N)]
+            send(K_YIM, 0, slot, mode)
+
+    def im_second(slot, mode):
+        recv(K_ZIM_U, 0, slot, mode)
+        recv(K_ZIM_D, 0, slot, mode)
+        for rows in [ALL] if mode == FIRST else rims_and_middle(mode)[0]:
+            a[1, 0, rows] = d[0, 1, 1, rows] + r[Z_IM, 0, slot, rows]
+        send(K_YIM_T, 0, slot, mode)
+        send(K_YIM_B, 0, slot, mode)
+        if mode == FIRST:
+            send(K_YIM, 0, slot, mode)
+
     def mid_back(s, slot, mode):
         recv(K_ZM_U, s, slot, mode)
         recv(K_ZM_D, s, slot, mode)
@@ -199,27 +259,34 @@
         send(K_P3, s, slot, mode)
 
     def finish(s, slot, mode):
-        recv(K_ZRE_U, s, slot, mode)
-        recv(K_ZRE_D, s, slot, mode)
+        for kind in (K_ZRE_U, K_ZRE_D, K_ZRE_U2, K_ZRE_D2):
+            recv(kind, s, slot, mode)
         objects[s][1, 0] = objects[s][1, 0] + (a[0, s] + r[Z_RE, s, slot])
-        recv(K_YIM, s, slot, mode)
+        for kind in (K_YIM, K_YIM_T, K_YIM_B):
+            recv(kind, s, slot, mode)
         objects[s][1, 1] = objects[s][1, 1] + (a[1, s] + r[Y_IM, s, slot])
         recv(K_P3, s, slot, mode)
-        for kind in range(10):
-            sent(kind, s, slot, mode)
+
+    def all_sent(slot, mode):
+        for s in range(2):
+            for kind in range(KINDS):
+                sent(kind, s, slot, mode)
 
     def exchange(slot, mode):
         mid_m(0, slot, mode)
         mid_m(1, slot, USUAL)
         mid_im(1, slot, mode)
-        mid_re(0, slot, mode)
-        mid_im(0, slot, mode)
+        re_first(slot, mode)
+        im_first(slot, mode)
+        re_second(slot, mode)
+        im_second(slot, mode)
         mid_re(1, slot, mode)
         mid_back(0, slot, mode)
         mid_back(1, slot, mode)
         if mode == LAST:
             finish(1, slot, mode)
             give(1)
+        all_sent(slot, mode)
         finish(0, slot, mode)
 
     def send_home(s):
@@ -328,8 +395,8 @@
     mid_m(0, 0, FIRST)
     begin(1)
     pass_start(*frames(0))
-    mid_re(0, 0, FIRST)
-    mid_im(0, 0, FIRST)
+    re_first(0, FIRST)
+    im_second(0, FIRST)
     mid_m(1, 0, FIRST)
     mid_back(0, 0, FIRST)
     mid_re(1, 0, FIRST)
@@ -337,6 +404,7 @@
     mid_back(1, 0, FIRST)
     for i in range(2):
         pass_wait(i, *inputs[i])
+    all_sent(0, FIRST)
     finish(0, 0, FIRST)
 
     def split(x):
@@ -360,7 +428,7 @@
         right = objects[s][hr, c, pl.ds(r0, N), :]
         return pltpu.roll(jnp.where(lane >= q0, left, right), (N - q0) & (N - 1), 1)
 
-    def scatter(s, places, grads):
+    def scatter(s, slot, places, grads):
         for m in range(BATCH):
             r0, q0, weight = places[m]
             fl = jnp.where(jnp.logical_and(lane >= q0, l_ok), weight, 0.0)
@@ -369,10 +437,13 @@
                 g = pltpu.roll(grads[c][m], q0 & (N - 1), 1)
                 z[m, 0, c, pl.ds(N, N)] = g * fl
                 z[m, 1, c, pl.ds(N, N)] = g * fr
-        for h, half in ((0, hl), (1, hr)):
-            for c in range(2):
-                total = z[0, h, c, pl.ds(N - places[0][0], 2 * N), :] + z[1, h, c, pl.ds(N - places[1][0], 2 * N), :]
-                d[s, half, c] = jnp.where(row_ok, total, 0.0)
+        for half, side, planes in ((1, core, ((0, (K_YRE, K_YRE_T, K_YRE_B)), (1, (K_ZIM_U2, K_ZIM_D2, K_ZIM_U, K_ZIM_D)))), (0, 1 - core, ((1 - core, (K_M,)), (core, ())))):
+            for c, kinds in planes:
+                first = z[0, side, c, pl.ds(N - places[0][0], 2 * N), :]
+                second = z[1, side, c, pl.ds(N - places[1][0], 2 * N), :]
+                d[s, half, c] = jnp.where(row_ok, first + second, 0.0)
+                for kind in kinds:
+                    send(kind, s, slot, USUAL)
 
     def batch(b, carry):
         slot = lax.rem(b + 1, 2)
@@ -411,15 +482,13 @@
         excess = [re[m] * re[m] + im[m] * im[m] - goal[m] for m in range(BATCH)]
         re, im = transform([excess[m] * re[m] for m in range(BATCH)], [excess[m] * im[m] for m in range(BATCH)], 1)
         both = [cmul(psi[m, 0], -psi[m, 1], re[m], im[m]) for m in range(BATCH)]
-        scatter(1, places, ([x for x, _ in both], [y for _, y in both]))
-        start(1, slot, USUAL)
+        scatter(1, slot, places, ([x for x, _ in both], [y for _, y in both]))
         both = [cmul(pat[m, 0], -pat[m, 1], re[m], im[m]) for m in range(BATCH)]
         re, im = transform([x for x, _ in both], [y for _, y in both], 0)
         both = [cmul(re[m], im[m], q[0], -q[1]) for m in range(BATCH)]
         re, im = transform([x for x, _ in both], [y for _, y in both], 1)
         both = [cmul(re[m], im[m], pr, -pi) for m in range(BATCH)]
-        scatter(0, places, ([x for x, _ in both], [y for _, y in both]))
-        start(0, slot, USUAL)
+        scatter(0, slot, places, ([x for x, _ in both], [y for _, y in both]))
         pl.when(b < NB - 1)(lambda: exchange(slot, USUAL))
         pl.when(b == NB - 1)(lambda: exchange(slot, LAST))
         return carry
@@ -462,8 +531,8 @@
                 pltpu.VMEM((2, 2, 2 * N, 2 * N), BF16),
                 pltpu.SMEM((2, NB * BATCH), jnp.int32),
                 pltpu.SMEM((1, 1), jnp.int32),
-                pltpu.SemaphoreType.DMA((10, 2, 2)),
-                pltpu.SemaphoreType.DMA((10, 2, 2)),
+                pltpu.SemaphoreType.DMA((KINDS, 2, 2)),
+                pltpu.SemaphoreType.DMA((KINDS, 2, 2)),
                 pltpu.SemaphoreType.DMA((4 + NB,)),
                 pltpu.SemaphoreType.DMA((4 + NB,)),
                 pltpu.SemaphoreType.DMA((2,)),

time: 113 us -> 112 us (level)
  no operation moved by 1% of the time
where the time goes in v6:
time: 112 us; the launch traced here: 110 us
  Pallas kernels  108 us (96%)
  local copies, waits for them, and re-layouts  1.67 us (1%)
    pallas_call x1, Pallas kernels, local(): pl.pallas_call(kernel, out_shape=jax.ShapeDtypeStruct((2, 2, N, N), F32),...  108 us

profile of v6, /device:TPU:6, one launch (start us, length us, event | category | flops | bytes accessed | tf_op | source)
XLA Modules:
  0.0 110.3 jit_solution(6821735098612228836)
XLA Ops:
  0.7 108.0 %shard_map.73 = f32[2,2,128,128]{3,2,1,0:T(8,128)} custom-call(s32[2,12]{1,0:T(2,128)} %bitcast.5, s32[1,1]{1,0:T(1,128)S(6)} %copy.9.cnt_in, f32[2,2,128,128]{3,2,1,0:T(8,128)} %obj.1, f32[2,128,128]{2,1,0:T(8,128)} %probe_in.1, f32[128,128]{1,0:T(8,128)} %prop_in.1, f32[12,128,128]{2,1,0:T(8,128)} %bitcast.4, bf16[2,2,256,256]{3,2,1,0:T(8,128)(2,1)} %constant.2.clone.w_in), custom_call_target="tpu_custom_call" | custom-call | tf_op jit(solution)/shard_map/pallas_call | solution.py:510
  108.7 1.7 %copy.10 = f32[2,2,128,128]{3,2,1,0:T(8,128)} copy(f32[2,2,128,128]{3,2,1,0:T(8,128)} %shard_map.73) | data formatting | bytes 524288

commit v7 on v6

--- a/solution.py
+++ b/solution.py
@@ -91,8 +91,6 @@
     hr = core
 
     lane = lax.broadcasted_iota(jnp.int32, (1, N), 1)
-    row = lax.broadcasted_iota(jnp.int32, (2 * N, N), 0)
-    row_ok = jnp.logical_and(row >= jnp.where(gx == 0, H, 0), row < jnp.where(gx == 7, 3 * H, 4 * H))
     l_ok = lane >= jnp.where(gy == 0, H, 0)
     r_ok = lane < jnp.where(gy == 15, H, N)
 
@@ -441,7 +439,16 @@
             for c, kinds in planes:
                 first = z[0, side, c, pl.ds(N - places[0][0], 2 * N), :]
                 second = z[1, side, c, pl.ds(N - places[1][0], 2 * N), :]
-                d[s, half, c] = jnp.where(row_ok, first + second, 0.0)
+                d[s, half, c] = first + second
+
+                @pl.when(gx == 0)
+                def _():
+                    d[s, half, c, pl.ds(0, H)] = jnp.zeros((H, N), F32)
+
+                @pl.when(gx == 7)
+                def _():
+                    d[s, half, c, pl.ds(3 * H, H)] = jnp.zeros((H, N), F32)
+
                 for kind in kinds:
                     send(kind, s, slot, USUAL)
 

time: 112 us -> 112 us (level)
  no operation moved by 1% of the time
where the time goes in v7:
time: 112 us; the launch traced here: 110 us
  Pallas kernels  108 us (96%)
  local copies, waits for them, and re-layouts  1.67 us (1%)
    pallas_call x1, Pallas kernels, local(): pl.pallas_call(kernel, out_shape=jax.ShapeDtypeStruct((2, 2, N, N), F32),...  108 us

profile of v7, /device:TPU:6, one launch (start us, length us, event | category | flops | bytes accessed | tf_op | source)
XLA Modules:
  0.0 110.4 jit_solution(7383991777772625253)
XLA Ops:
  0.7 108.1 %shard_map.73 = f32[2,2,128,128]{3,2,1,0:T(8,128)} custom-call(s32[2,12]{1,0:T(2,128)} %bitcast.5, s32[1,1]{1,0:T(1,128)S(6)} %copy.9.cnt_in, f32[2,2,128,128]{3,2,1,0:T(8,128)} %obj.1, f32[2,128,128]{2,1,0:T(8,128)} %probe_in.1, f32[128,128]{1,0:T(8,128)} %prop_in.1, f32[12,128,128]{2,1,0:T(8,128)} %bitcast.4, bf16[2,2,256,256]{3,2,1,0:T(8,128)(2,1)} %constant.2.clone.w_in), custom_call_target="tpu_custom_call" | custom-call | tf_op jit(solution)/shard_map/pallas_call | solution.py:517
  108.7 1.7 %copy.10 = f32[2,2,128,128]{3,2,1,0:T(8,128)} copy(f32[2,2,128,128]{3,2,1,0:T(8,128)} %shard_map.73) | data formatting | bytes 524288
